TPU v7x, 512 devices: a whole 4x8x8 slice. The times are simulated.
512 devices in a mesh: seq: 128 (over z, y, x_lo), head: 4 (over x_hi, core).
Axes of the slice: x: 4 (x_hi: 2, x_lo: 2; x = x_hi * 2 + x_lo), y: 8, z: 8, core: 2. Of those that a mesh axis runs over, the one named last changes fastest.
Arguments:
- queries: bfloat16 [32768, 32, 128], P(('seq', 'head')), may hold values from -3 to 3
- key_vectors: bfloat16 [32768, 32, 128], P(('seq', 'head')), may hold values from -3 to 3
- value_vectors: bfloat16 [32768, 32, 128], P(('seq', 'head')), may hold values from -4 to 4
- grad_output: bfloat16 [32768, 32, 128], P(('seq', 'head')), may hold values from -4 to 4
- logsumexp: float32 [32, 32768], P('head', 'seq'), may hold values from 2 to 4
- row_delta: float32 [32, 32768], P('head', 'seq'), may hold values from -16 to 16
Outputs:
- grad_queries: bfloat16 [32768, 32, 128], P(('seq', 'head'))
- grad_keys: bfloat16 [32768, 32, 128], P(('seq', 'head'))
- grad_values: bfloat16 [32768, 32, 128], P(('seq', 'head'))
All inputs are finite; a program needn't handle non-finite values.
Results may differ from a plain program's by a relative error of at most 0.02.
Values may be sent and summed in bfloat16 or wider, within the bound.
A program may use at most 64 MiB of HBM per device.

v0:
```python
import jax
import jax.numpy as jnp
from jax import lax
from jax.sharding import PartitionSpec as P

STEPS = 4


def shifted(block, axis, distance):
    devices = range(lax.axis_size(axis))
    route = [((i - distance) % len(devices), i) for i in devices]
    return lax.ppermute(block, axis, route)


def token_places(device, seq_count, half_rows):
    offsets = jnp.arange(half_rows, dtype=jnp.int32)
    first = device * half_rows + offsets
    second = (2 * seq_count - 1 - device) * half_rows + offsets
    return jnp.concatenate([first, second])


def tile_grads(q_rows, g_rows, lse_rows, delta_rows, k_rows, v_rows, causal, scaling):
    scores = (
        jnp.einsum("qhd,khd->hqk", q_rows, k_rows, preferred_element_type=jnp.float32) * scaling
    )
    probs = jnp.where(causal[None], jnp.exp(scores - lse_rows[:, :, None]), 0.0)
    v_grad = jnp.einsum(
        "hqk,qhd->khd", probs.astype(jnp.bfloat16), g_rows, preferred_element_type=jnp.float32
    )
    p_grad = jnp.einsum("qhd,khd->hqk", g_rows, v_rows, preferred_element_type=jnp.float32)
    s_grad = (probs * (p_grad - delta_rows[:, :, None])).astype(jnp.bfloat16)
    q_grad = (
        jnp.einsum("hqk,khd->qhd", s_grad, k_rows, preferred_element_type=jnp.float32) * scaling
    )
    k_grad = (
        jnp.einsum("hqk,qhd->khd", s_grad, q_rows, preferred_element_type=jnp.float32) * scaling
    )
    return (q_grad.astype(jnp.bfloat16), k_grad.astype(jnp.bfloat16), v_grad.astype(jnp.bfloat16))


def pair_grads(
    q_rows, g_rows, lse_rows, delta_rows, k_rows, v_rows, q_device, k_device, seq_count, diagonal
):
    half_rows = q_rows.shape[0] // 2
    scaling = q_rows.shape[2] ** (-0.5)
    q_places = token_places(q_device, seq_count, half_rows)
    k_places = token_places(k_device, seq_count, half_rows)
    causal = k_places[None, :] <= q_places[:, None]
    if diagonal:
        return tile_grads(q_rows, g_rows, lse_rows, delta_rows, k_rows, v_rows, causal, scaling)
    return tile_grads(q_rows, g_rows, lse_rows, delta_rows, k_rows, v_rows, causal, scaling)


def on_device(queries, key_vectors, value_vectors, grad_output, logsumexp, row_delta):
    q_local, k_local, v_local, g_local = (
        lax.all_to_all(queries, "head", split_axis=1, concat_axis=0, tiled=True),
        lax.all_to_all(key_vectors, "head", split_axis=1, concat_axis=0, tiled=True),
        lax.all_to_all(value_vectors, "head", split_axis=1, concat_axis=0, tiled=True),
        lax.all_to_all(grad_output, "head", split_axis=1, concat_axis=0, tiled=True),
    )
    seq_count = lax.axis_size("seq")
    myself = lax.axis_index("seq")
    grad_shape = q_local.shape
    q_total = jnp.zeros(grad_shape, jnp.float32)
    k_total = jnp.zeros(grad_shape, jnp.float32)
    v_total = jnp.zeros(grad_shape, jnp.float32)
    k_visit, v_visit = (k_local, v_local)
    for distance in range(STEPS):
        if distance > 0:
            k_visit, v_visit = shifted((k_visit, v_visit), "seq", 1)
        source = (myself - distance) % seq_count
        q_part, k_part, v_part = pair_grads(
            q_local,
            g_local,
            logsumexp,
            row_delta,
            k_visit,
            v_visit,
            myself,
            source,
            seq_count,
            distance == 0,
        )
        q_total = q_total + q_part.astype(jnp.float32)
        if distance > 0:
            k_part, v_part = shifted((k_part, v_part), "seq", -distance)
        k_total = k_total + k_part.astype(jnp.float32)
        v_total = v_total + v_part.astype(jnp.float32)
    q_final = q_total.astype(jnp.bfloat16)
    k_final = k_total.astype(jnp.bfloat16)
    v_final = v_total.astype(jnp.bfloat16)
    return (
        lax.all_to_all(q_final, "head", split_axis=0, concat_axis=1, tiled=True),
        lax.all_to_all(k_final, "head", split_axis=0, concat_axis=1, tiled=True),
        lax.all_to_all(v_final, "head", split_axis=0, concat_axis=1, tiled=True),
    )


def solution(mesh):
    placed = (
        P(("seq", "head"), None, None),
        P(("seq", "head"), None, None),
        P(("seq", "head"), None, None),
        P(("seq", "head"), None, None),
        P("head", "seq"),
        P("head", "seq"),
    )
    return jax.shard_map(
        on_device,
        mesh=mesh,
        in_specs=placed,
        out_specs=(
            P(("seq", "head"), None, None),
            P(("seq", "head"), None, None),
            P(("seq", "head"), None, None),
        ),
        check_vma=False,
    )
```

profile of v0, /device:TPU:1, one launch (start us, length us, event | category | flops | bytes accessed | tf_op | source)
XLA Modules:
  0.0 262.2 jit_solution(15272329574161554548)
XLA Ops:
  0.7 2.2 copy.24
  2.8 10.3 %all-to-all-start = ((bf16[64,32,128]{2,0,1:T(8,128)(2,1)}), bf16[64,32,128]{2,0,1:T(8,128)(2,1)S(1)}, u32[]{:S(2)}, u32[]{:S(2)}) async-start(bf16[64,32,128]{2,0,1:T(8,128)(2,1)} %copy.24), calls=%async_computation | async-start | bytes 1048576 | tf_op jit(solution)/shard_map/all_to_all | solution.py:56
  13.1 1.0 copy.26
  14.1 1.0 copy.30
  15.1 1.0 copy.28
  16.1 6.5 %all-to-all-done = bf16[64,32,128]{2,0,1:T(8,128)(2,1)S(1)} async-done(((bf16[64,32,128]{2,0,1:T(8,128)(2,1)}), bf16[64,32,128]{2,0,1:T(8,128)(2,1)S(1)}, u32[]{:S(2)}, u32[]{:S(2)}) %all-to-all-start) | async-done | bytes 524320 | tf_op jit(solution)/shard_map/all_to_all | solution.py:56
  22.6 4.3 %all-to-all-start.1 = ((bf16[64,32,128]{2,0,1:T(8,128)(2,1)}), bf16[64,32,128]{2,0,1:T(8,128)(2,1)S(1)}, u32[]{:S(2)}, u32[]{:S(2)}) async-start(bf16[64,32,128]{2,0,1:T(8,128)(2,1)} %copy.26), calls=%async_computation.1 | async-start | bytes 1048576 | tf_op jit(solution)/shard_map/all_to_all | solution.py:57
  27.0 9.4 %all-to-all-done.1 = bf16[64,32,128]{2,0,1:T(8,128)(2,1)S(1)} async-done(((bf16[64,32,128]{2,0,1:T(8,128)(2,1)}), bf16[64,32,128]{2,0,1:T(8,128)(2,1)S(1)}, u32[]{:S(2)}, u32[]{:S(2)}) %all-to-all-start.1) | async-done | bytes 524320 | tf_op jit(solution)/shard_map/all_to_all | solution.py:57
  36.4 4.3 %all-to-all-start.3 = ((bf16[64,32,128]{2,0,1:T(8,128)(2,1)}), bf16[64,32,128]{2,0,1:T(8,128)(2,1)S(1)}, u32[]{:S(2)}, u32[]{:S(2)}) async-start(bf16[64,32,128]{2,0,1:T(8,128)(2,1)} %copy.30), calls=%async_computation.3 | async-start | bytes 1048576 | tf_op jit(solution)/shard_map/all_to_all | solution.py:58
  40.8 9.4 %all-to-all-done.3 = bf16[64,32,128]{2,0,1:T(8,128)(2,1)S(1)} async-done(((bf16[64,32,128]{2,0,1:T(8,128)(2,1)}), bf16[64,32,128]{2,0,1:T(8,128)(2,1)S(1)}, u32[]{:S(2)}, u32[]{:S(2)}) %all-to-all-start.3) | async-done | bytes 524320 | tf_op jit(solution)/shard_map/all_to_all | solution.py:58
  50.2 4.3 %all-to-all-start.2 = ((bf16[64,32,128]{2,0,1:T(8,128)(2,1)}), bf16[64,32,128]{2,0,1:T(8,128)(2,1)S(1)}, u32[]{:S(2)}, u32[]{:S(2)}) async-start(bf16[64,32,128]{2,0,1:T(8,128)(2,1)} %copy.28), calls=%async_computation.2 | async-start | bytes 1048576 | tf_op jit(solution)/shard_map/all_to_all | solution.py:59
  54.5 0.2 broadcast_compare_fusion
  54.9 0.8 copy.31
  55.7 8.3 %all-to-all-done.2 = bf16[64,32,128]{2,0,1:T(8,128)(2,1)S(1)} async-done(((bf16[64,32,128]{2,0,1:T(8,128)(2,1)}), bf16[64,32,128]{2,0,1:T(8,128)(2,1)S(1)}, u32[]{:S(2)}, u32[]{:S(2)}) %all-to-all-start.2) | async-done | bytes 524320 | tf_op jit(solution)/shard_map/all_to_all | solution.py:59
  64.0 1.9 collective-permute-start.1
  66.0 1.9 collective-permute-start
  67.9 0.8 exponential_select_fusion.3
  68.7 1.9 multiply_convert_fusion.3
  70.6 0.4 fusion.19
  71.1 25.0 %collective-permute-done = bf16[256,8,128]{2,0,1:T(8,128)(2,1)S(1)} collective-permute-done((bf16[256,8,128]{2,0,1:T(8,128)(2,1)S(1)}, bf16[256,8,128]{2,0,1:T(8,128)(2,1)S(1)}, u32[]{:S(2)}, u32[]{:S(2)}) %collective-permute-start) | collective-permute-done | bytes 524320 | tf_op jit(solution)/shard_map/ppermute | solution.py:12
  96.0 0.8 exponential_select_fusion.2
  96.8 0.4 multiply_convert_fusion.2
  97.3 1.3 fusion.26
  98.6 3.0 %collective-permute-start.6 = (bf16[256,8,128]{2,0,1:T(8,128)(2,1)}, bf16[256,8,128]{2,0,1:T(8,128)(2,1)S(1)}, u32[]{:S(2)}, u32[]{:S(2)}) collective-permute-start(bf16[256,8,128]{2,0,1:T(8,128)(2,1)} %fusion.26), channel_id=1, source_target_pairs={{4,0},{8,4},{12,8},{16,12},{20,16},{24,20},{28,24},{32,28},{36,32}... | collective-permute-start | bytes 1572872 | tf_op jit(solution)/shard_map/ppermute | solution.py:12
  101.6 2.2 collective-permute-start.2
  103.9 0.5 fusion.21
  104.4 7.3 %collective-permute-start.9 = (bf16[256,8,128]{2,0,1:T(8,128)(2,1)S(1)}, bf16[256,8,128]{2,0,1:T(8,128)(2,1)S(1)}, u32[]{:S(2)}, u32[]{:S(2)}) collective-permute-start(bf16[256,8,128]{2,0,1:T(8,128)(2,1)S(1)} %fusion.21), channel_id=1, source_target_pairs={{4,0},{8,4},{12,8},{16,12},{20,16},{24,20},{28,24},{32,28},{36,32}... | collective-permute-start | bytes 1572872 | tf_op jit(solution)/shard_map/ppermute | solution.py:12
  111.7 1.9 collective-permute-start.3
  113.6 0.4 fusion.18
  114.0 15.9 %collective-permute-done.2 = bf16[256,8,128]{2,0,1:T(8,128)(2,1)S(1)} collective-permute-done((bf16[256,8,128]{2,0,1:T(8,128)(2,1)S(1)}, bf16[256,8,128]{2,0,1:T(8,128)(2,1)S(1)}, u32[]{:S(2)}, u32[]{:S(2)}) %collective-permute-start.2) | collective-permute-done | bytes 524320 | tf_op jit(solution)/shard_map/ppermute | solution.py:12
  129.9 0.8 exponential_select_fusion.1
  130.7 10.5 %collective-permute-done.3 = bf16[256,8,128]{2,0,1:T(8,128)(2,1)S(1)} collective-permute-done((bf16[256,8,128]{2,0,1:T(8,128)(2,1)S(1)}, bf16[256,8,128]{2,0,1:T(8,128)(2,1)S(1)}, u32[]{:S(2)}, u32[]{:S(2)}) %collective-permute-start.3) | collective-permute-done | bytes 524320 | tf_op jit(solution)/shard_map/ppermute | solution.py:12
  141.2 0.4 multiply_convert_fusion.1
  141.6 1.3 fusion.25
  142.9 11.3 %collective-permute-start.7 = (bf16[256,8,128]{2,0,1:T(8,128)(2,1)}, bf16[256,8,128]{2,0,1:T(8,128)(2,1)}, u32[]{:S(2)}, u32[]{:S(2)}) collective-permute-start(bf16[256,8,128]{2,0,1:T(8,128)(2,1)} %fusion.25), channel_id=1, source_target_pairs={{8,0},{12,4},{16,8},{20,12},{24,16},{28,20},{32,24},{36,28},{40,32... | collective-permute-start | bytes 1572872 | tf_op jit(solution)/shard_map/ppermute | solution.py:12
  154.2 4.1 %collective-permute-start.4 = (bf16[256,8,128]{2,0,1:T(8,128)(2,1)S(1)}, bf16[256,8,128]{2,0,1:T(8,128)(2,1)S(1)}, u32[]{:S(2)}, u32[]{:S(2)}) collective-permute-start(bf16[256,8,128]{2,0,1:T(8,128)(2,1)S(1)} %collective-permute-done.2), channel_id=1, source_target_pairs={{508,0},{0,4},{4,8},{8,12},{12,16},{16,20},{20,24},{24,28},{28,32}... | collective-permute-start | bytes 1572872 | tf_op jit(solution)/shard_map/ppermute | solution.py:12
  158.4 1.3 fusion.22
  159.7 1.9 collective-permute-start.10
  161.6 0.4 fusion.16
  162.0 10.4 %collective-permute-done.4 = bf16[256,8,128]{2,0,1:T(8,128)(2,1)S(1)} collective-permute-done((bf16[256,8,128]{2,0,1:T(8,128)(2,1)S(1)}, bf16[256,8,128]{2,0,1:T(8,128)(2,1)S(1)}, u32[]{:S(2)}, u32[]{:S(2)}) %collective-permute-start.4) | collective-permute-done | bytes 524320 | tf_op jit(solution)/shard_map/ppermute | solution.py:12
  172.4 1.9 collective-permute-start.5
  174.3 0.8 exponential_select_fusion
  175.1 1.3 fusion.23
  176.5 13.2 %collective-permute-done.5 = bf16[256,8,128]{2,0,1:T(8,128)(2,1)S(1)} collective-permute-done((bf16[256,8,128]{2,0,1:T(8,128)(2,1)S(1)}, bf16[256,8,128]{2,0,1:T(8,128)(2,1)S(1)}, u32[]{:S(2)}, u32[]{:S(2)}) %collective-permute-start.5) | collective-permute-done | bytes 524320 | tf_op jit(solution)/shard_map/ppermute | solution.py:12
  189.7 1.9 collective-permute-start.11
  191.6 0.4 multiply_convert_fusion
  192.0 1.3 fusion.24
  193.3 1.9 collective-permute-start.8
  195.3 0.4 fusion.20
  195.7 1.1 copy.32
  196.8 6.6 %all-to-all-start.4 = ((bf16[256,8,128]{2,1,0:T(8,128)(2,1)}), bf16[256,8,128]{2,1,0:T(8,128)(2,1)S(1)}, u32[]{:S(2)}, u32[]{:S(2)}) async-start(bf16[256,8,128]{2,1,0:T(8,128)(2,1)} %copy.32), calls=%async_computation.4 | async-start | bytes 1048576 | tf_op jit(solution)/shard_map/all_to_all | solution.py:93
  203.5 12.3 %collective-permute-done.11 = bf16[256,8,128]{2,0,1:T(8,128)(2,1)} collective-permute-done((bf16[256,8,128]{2,0,1:T(8,128)(2,1)}, bf16[256,8,128]{2,0,1:T(8,128)(2,1)}, u32[]{:S(2)}, u32[]{:S(2)}) %collective-permute-start.11) | collective-permute-done | bytes 524320 | tf_op jit(solution)/shard_map/ppermute | solution.py:12
  215.8 2.5 add_convert_fusion
  218.3 1.1 copy.44
  219.4 14.6 %all-to-all-done.4 = bf16[256,8,128]{2,1,0:T(8,128)(2,1)S(1)} async-done(((bf16[256,8,128]{2,1,0:T(8,128)(2,1)}), bf16[256,8,128]{2,1,0:T(8,128)(2,1)S(1)}, u32[]{:S(2)}, u32[]{:S(2)}) %all-to-all-start.4) | async-done | bytes 524320 | tf_op jit(solution)/shard_map/all_to_all | solution.py:93
  234.0 4.0 %all-to-all-start.6 = ((bf16[256,8,128]{2,1,0:T(8,128)(2,1)}), bf16[256,8,128]{2,1,0:T(8,128)(2,1)S(1)}, u32[]{:S(2)}, u32[]{:S(2)}) async-start(bf16[256,8,128]{2,1,0:T(8,128)(2,1)} %copy.44), calls=%async_computation.6 | async-start | bytes 1048576 | tf_op jit(solution)/shard_map/all_to_all | solution.py:95
  238.1 1.8 add_convert_fusion.1
  239.8 1.1 copy.38
  241.0 6.6 %all-to-all-done.6 = bf16[256,8,128]{2,1,0:T(8,128)(2,1)S(1)} async-done(((bf16[256,8,128]{2,1,0:T(8,128)(2,1)}), bf16[256,8,128]{2,1,0:T(8,128)(2,1)S(1)}, u32[]{:S(2)}, u32[]{:S(2)}) %all-to-all-start.6) | async-done | bytes 524320 | tf_op jit(solution)/shard_map/all_to_all | solution.py:95
  247.5 4.3 %all-to-all-start.5 = ((bf16[256,8,128]{2,1,0:T(8,128)(2,1)}), bf16[256,8,128]{2,1,0:T(8,128)(2,1)S(1)}, u32[]{:S(2)}, u32[]{:S(2)}) async-start(bf16[256,8,128]{2,1,0:T(8,128)(2,1)} %copy.38), calls=%async_computation.5 | async-start | bytes 1048576 | tf_op jit(solution)/shard_map/all_to_all | solution.py:94
  251.8 0.9 copy.59
  252.7 0.9 copy.57
  253.6 7.7 %all-to-all-done.5 = bf16[256,8,128]{2,1,0:T(8,128)(2,1)S(1)} async-done(((bf16[256,8,128]{2,1,0:T(8,128)(2,1)}), bf16[256,8,128]{2,1,0:T(8,128)(2,1)S(1)}, u32[]{:S(2)}, u32[]{:S(2)}) %all-to-all-start.5) | async-done | bytes 524320 | tf_op jit(solution)/shard_map/all_to_all | solution.py:94
  261.3 0.9 copy.58
  (33 shorter events, 0.2 us)
Async XLA Ops:
  0.6 12.5 %copy-start.2 = (bf16[64,32,128]{2,1,0:T(8,128)(2,1)S(1)}, bf16[64,32,128]{2,1,0:T(8,128)(2,1)}, u32[]{:S(2)}) copy-start(bf16[64,32,128]{2,1,0:T(8,128)(2,1)} %param.7) | copy-start | bytes 1572868
  0.6 13.5 %copy-start.3 = (bf16[64,32,128]{2,1,0:T(8,128)(2,1)S(1)}, bf16[64,32,128]{2,1,0:T(8,128)(2,1)}, u32[]{:S(2)}) copy-start(bf16[64,32,128]{2,1,0:T(8,128)(2,1)} %param.8) | copy-start | bytes 1572868
  0.7 14.5 %copy-start.4 = (bf16[64,32,128]{2,1,0:T(8,128)(2,1)S(1)}, bf16[64,32,128]{2,1,0:T(8,128)(2,1)}, u32[]{:S(2)}) copy-start(bf16[64,32,128]{2,1,0:T(8,128)(2,1)} %param.9) | copy-start | bytes 1572868
  2.8 19.8 %all-to-all-start = ((bf16[64,32,128]{2,0,1:T(8,128)(2,1)}), bf16[64,32,128]{2,0,1:T(8,128)(2,1)S(1)}, u32[]{:S(2)}, u32[]{:S(2)}) async-start(bf16[64,32,128]{2,0,1:T(8,128)(2,1)} %copy.24), calls=%async_computation | async-start | bytes 1048576 | tf_op jit(solution)/shard_map/all_to_all | solution.py:56
  22.6 13.8 %all-to-all-start.1 = ((bf16[64,32,128]{2,0,1:T(8,128)(2,1)}), bf16[64,32,128]{2,0,1:T(8,128)(2,1)S(1)}, u32[]{:S(2)}, u32[]{:S(2)}) async-start(bf16[64,32,128]{2,0,1:T(8,128)(2,1)} %copy.26), calls=%async_computation.1 | async-start | bytes 1048576 | tf_op jit(solution)/shard_map/all_to_all | solution.py:57
  36.4 13.8 %all-to-all-start.3 = ((bf16[64,32,128]{2,0,1:T(8,128)(2,1)}), bf16[64,32,128]{2,0,1:T(8,128)(2,1)S(1)}, u32[]{:S(2)}, u32[]{:S(2)}) async-start(bf16[64,32,128]{2,0,1:T(8,128)(2,1)} %copy.30), calls=%async_computation.3 | async-start | bytes 1048576 | tf_op jit(solution)/shard_map/all_to_all | solution.py:58
  50.2 13.8 %all-to-all-start.2 = ((bf16[64,32,128]{2,0,1:T(8,128)(2,1)}), bf16[64,32,128]{2,0,1:T(8,128)(2,1)S(1)}, u32[]{:S(2)}, u32[]{:S(2)}) async-start(bf16[64,32,128]{2,0,1:T(8,128)(2,1)} %copy.28), calls=%async_computation.2 | async-start | bytes 1048576 | tf_op jit(solution)/shard_map/all_to_all | solution.py:59
  54.8 13.2 %copy-start.6 = (f32[8,256]{1,0:T(8,128)S(1)}, f32[8,256]{1,0:T(8,128)}, u32[]{:S(2)}) copy-start(f32[8,256]{1,0:T(8,128)} %param.10) | copy-start | bytes 24580
  64.0 4.7 %copy-start.5 = (f32[8,256]{1,0:T(8,128)S(1)}, f32[8,256]{1,0:T(8,128)}, u32[]{:S(2)}) copy-start(f32[8,256]{1,0:T(8,128)} %param.11) | copy-start | bytes 24580
  64.0 32.8 %collective-permute-start.1 = (bf16[256,8,128]{2,0,1:T(8,128)(2,1)}, bf16[256,8,128]{2,0,1:T(8,128)(2,1)S(1)}, u32[]{:S(2)}, u32[]{:S(2)}) collective-permute-start(bf16[256,8,128]{2,0,1:T(8,128)(2,1)} %bitcast.11), channel_id=1, source_target_pairs={{508,0},{0,4},{4,8},{8,12},{12,16},{16,20},{20,24},{24,28},{28,32}... | collective-permute-start | bytes 1572872 | tf_op jit(solution)/shard_map/ppermute | solution.py:12
  66.0 30.1 %collective-permute-start = (bf16[256,8,128]{2,0,1:T(8,128)(2,1)S(1)}, bf16[256,8,128]{2,0,1:T(8,128)(2,1)S(1)}, u32[]{:S(2)}, u32[]{:S(2)}) collective-permute-start(bf16[256,8,128]{2,0,1:T(8,128)(2,1)S(1)} %bitcast.108), channel_id=1, source_target_pairs={{508,0},{0,4},{4,8},{8,12},{12,16},{16,20},{20,24},{24,28},{28,32}... | collective-permute-start | bytes 1572872 | tf_op jit(solution)/shard_map/ppermute | solution.py:12
  68.7 1.9 copy-start
  98.6 139.5 %collective-permute-start.6 = (bf16[256,8,128]{2,0,1:T(8,128)(2,1)}, bf16[256,8,128]{2,0,1:T(8,128)(2,1)S(1)}, u32[]{:S(2)}, u32[]{:S(2)}) collective-permute-start(bf16[256,8,128]{2,0,1:T(8,128)(2,1)} %fusion.26), channel_id=1, source_target_pairs={{4,0},{8,4},{12,8},{16,12},{20,16},{24,20},{28,24},{32,28},{36,32}... | collective-permute-start | bytes 1572872 | tf_op jit(solution)/shard_map/ppermute | solution.py:12
  101.6 28.3 %collective-permute-start.2 = (bf16[256,8,128]{2,0,1:T(8,128)(2,1)S(1)}, bf16[256,8,128]{2,0,1:T(8,128)(2,1)S(1)}, u32[]{:S(2)}, u32[]{:S(2)}) collective-permute-start(bf16[256,8,128]{2,0,1:T(8,128)(2,1)S(1)} %collective-permute-done), channel_id=1, source_target_pairs={{508,0},{0,4},{4,8},{8,12},{12,16},{16,20},{20,24},{24,28},{28,32}... | collective-permute-start | bytes 1572872 | tf_op jit(solution)/shard_map/ppermute | solution.py:12
  104.4 89.0 %collective-permute-start.9 = (bf16[256,8,128]{2,0,1:T(8,128)(2,1)S(1)}, bf16[256,8,128]{2,0,1:T(8,128)(2,1)S(1)}, u32[]{:S(2)}, u32[]{:S(2)}) collective-permute-start(bf16[256,8,128]{2,0,1:T(8,128)(2,1)S(1)} %fusion.21), channel_id=1, source_target_pairs={{4,0},{8,4},{12,8},{16,12},{20,16},{24,20},{28,24},{32,28},{36,32}... | collective-permute-start | bytes 1572872 | tf_op jit(solution)/shard_map/ppermute | solution.py:12
  111.7 29.5 %collective-permute-start.3 = (bf16[256,8,128]{2,0,1:T(8,128)(2,1)S(1)}, bf16[256,8,128]{2,0,1:T(8,128)(2,1)S(1)}, u32[]{:S(2)}, u32[]{:S(2)}) collective-permute-start(bf16[256,8,128]{2,0,1:T(8,128)(2,1)S(1)} %collective-permute-done.1), channel_id=1, source_target_pairs={{508,0},{0,4},{4,8},{8,12},{12,16},{16,20},{20,24},{24,28},{28,32}... | collective-permute-start | bytes 1572872 | tf_op jit(solution)/shard_map/ppermute | solution.py:12
  142.9 95.1 %collective-permute-start.7 = (bf16[256,8,128]{2,0,1:T(8,128)(2,1)}, bf16[256,8,128]{2,0,1:T(8,128)(2,1)}, u32[]{:S(2)}, u32[]{:S(2)}) collective-permute-start(bf16[256,8,128]{2,0,1:T(8,128)(2,1)} %fusion.25), channel_id=1, source_target_pairs={{8,0},{12,4},{16,8},{20,12},{24,16},{28,20},{32,24},{36,28},{40,32... | collective-permute-start | bytes 1572872 | tf_op jit(solution)/shard_map/ppermute | solution.py:12
  154.2 18.2 %collective-permute-start.4 = (bf16[256,8,128]{2,0,1:T(8,128)(2,1)S(1)}, bf16[256,8,128]{2,0,1:T(8,128)(2,1)S(1)}, u32[]{:S(2)}, u32[]{:S(2)}) collective-permute-start(bf16[256,8,128]{2,0,1:T(8,128)(2,1)S(1)} %collective-permute-done.2), channel_id=1, source_target_pairs={{508,0},{0,4},{4,8},{8,12},{12,16},{16,20},{20,24},{24,28},{28,32}... | collective-permute-start | bytes 1572872 | tf_op jit(solution)/shard_map/ppermute | solution.py:12
  159.7 43.8 %collective-permute-start.10 = (bf16[256,8,128]{2,0,1:T(8,128)(2,1)}, bf16[256,8,128]{2,0,1:T(8,128)(2,1)}, u32[]{:S(2)}, u32[]{:S(2)}) collective-permute-start(bf16[256,8,128]{2,0,1:T(8,128)(2,1)} %fusion.22), channel_id=1, source_target_pairs={{8,0},{12,4},{16,8},{20,12},{24,16},{28,20},{32,24},{36,28},{40,32... | collective-permute-start | bytes 1572872 | tf_op jit(solution)/shard_map/ppermute | solution.py:12
  172.4 17.2 %collective-permute-start.5 = (bf16[256,8,128]{2,0,1:T(8,128)(2,1)S(1)}, bf16[256,8,128]{2,0,1:T(8,128)(2,1)S(1)}, u32[]{:S(2)}, u32[]{:S(2)}) collective-permute-start(bf16[256,8,128]{2,0,1:T(8,128)(2,1)S(1)} %collective-permute-done.3), channel_id=1, source_target_pairs={{508,0},{0,4},{4,8},{8,12},{12,16},{16,20},{20,24},{24,28},{28,32}... | collective-permute-start | bytes 1572872 | tf_op jit(solution)/shard_map/ppermute | solution.py:12
  189.7 26.1 %collective-permute-start.11 = (bf16[256,8,128]{2,0,1:T(8,128)(2,1)}, bf16[256,8,128]{2,0,1:T(8,128)(2,1)}, u32[]{:S(2)}, u32[]{:S(2)}) collective-permute-start(bf16[256,8,128]{2,0,1:T(8,128)(2,1)} %fusion.23), channel_id=1, source_target_pairs={{12,0},{16,4},{20,8},{24,12},{28,16},{32,20},{36,24},{40,28},{44,3... | collective-permute-start | bytes 1572872 | tf_op jit(solution)/shard_map/ppermute | solution.py:12
  193.3 2.4 copy-start.1
  193.3 44.7 %collective-permute-start.8 = (bf16[256,8,128]{2,0,1:T(8,128)(2,1)}, bf16[256,8,128]{2,0,1:T(8,128)(2,1)}, u32[]{:S(2)}, u32[]{:S(2)}) collective-permute-start(bf16[256,8,128]{2,0,1:T(8,128)(2,1)} %fusion.24), channel_id=1, source_target_pairs={{12,0},{16,4},{20,8},{24,12},{28,16},{32,20},{36,24},{40,28},{44,3... | collective-permute-start | bytes 1572872 | tf_op jit(solution)/shard_map/ppermute | solution.py:12
  196.8 37.2 %all-to-all-start.4 = ((bf16[256,8,128]{2,1,0:T(8,128)(2,1)}), bf16[256,8,128]{2,1,0:T(8,128)(2,1)S(1)}, u32[]{:S(2)}, u32[]{:S(2)}) async-start(bf16[256,8,128]{2,1,0:T(8,128)(2,1)} %copy.32), calls=%async_computation.4 | async-start | bytes 1048576 | tf_op jit(solution)/shard_map/all_to_all | solution.py:93
  234.0 13.5 %all-to-all-start.6 = ((bf16[256,8,128]{2,1,0:T(8,128)(2,1)}), bf16[256,8,128]{2,1,0:T(8,128)(2,1)S(1)}, u32[]{:S(2)}, u32[]{:S(2)}) async-start(bf16[256,8,128]{2,1,0:T(8,128)(2,1)} %copy.44), calls=%async_computation.6 | async-start | bytes 1048576 | tf_op jit(solution)/shard_map/all_to_all | solution.py:95
  247.5 13.8 %all-to-all-start.5 = ((bf16[256,8,128]{2,1,0:T(8,128)(2,1)}), bf16[256,8,128]{2,1,0:T(8,128)(2,1)S(1)}, u32[]{:S(2)}, u32[]{:S(2)}) async-start(bf16[256,8,128]{2,1,0:T(8,128)(2,1)} %copy.38), calls=%async_computation.5 | async-start | bytes 1048576 | tf_op jit(solution)/shard_map/all_to_all | solution.py:94
where the time goes:
time: 263 us; the launch traced here: 262 us
  waiting for transfers between devices  150 us (57%)
  starting transfers between devices  79.6 us (30%)
  matrix products  19.4 us (7%)
  local copies, waits for them, and re-layouts  12.2 us (5%)
    ppermute x12, waiting for transfers between devices, shifted(): return lax.ppermute(block, axis, route)  87.3 us
    ppermute x12, starting transfers between devices, shifted(): return lax.ppermute(block, axis, route)  41.4 us
    all_to_all x1, waiting for transfers between devices, on_device(): lax.all_to_all(q_final, 'head', split_axis=0, concat_axis=1, tiled=True)  14.6 us
    all_to_all x1, starting transfers between devices, on_device(): lax.all_to_all(queries, 'head', split_axis=1, concat_axis=0, tiled=True)  10.3 us
    all_to_all x1, waiting for transfers between devices, on_device(): lax.all_to_all(key_vectors, 'head', split_axis=1, concat_axis=0, tiled=True)  9.44 us
    all_to_all x1, waiting for transfers between devices, on_device(): lax.all_to_all(value_vectors, 'head', split_axis=1, concat_axis=0, tiled=...  9.44 us
    all_to_all x1, waiting for transfers between devices, on_device(): lax.all_to_all(grad_output, 'head', split_axis=1, concat_axis=0, tiled=True)  8.31 us
    all_to_all x1, waiting for transfers between devices, on_device(): lax.all_to_all(k_final, 'head', split_axis=0, concat_axis=1, tiled=True)  7.72 us
  transfers between devices with their start and end apart: 19, of which 13 were waited for; matrix products, arithmetic and copies ran while one was open for 10% of the time, Pallas kernels for 0%

commit v1 on v0

v1 whole, which is shorter than its diff:
```python
import math

import jax
import jax.numpy as jnp
from jax import lax
from jax.experimental import pallas as pl
from jax.experimental.pallas import tpu as pltpu
from jax.sharding import PartitionSpec as P

MESH = pl.DeviceIdType.MESH
GROUP = 8
BF16, F32 = jnp.bfloat16, jnp.float32
NT = (((1,), (1,)), ((), ()))
NN = (((1,), (0,)), ((), ()))
TN = (((0,), (0,)), ((), ()))


def dot(a, b, dims):
    return lax.dot_general(a, b, dims, preferred_element_type=F32)


def kernel(
    rows_total, q_ref, k_ref, v_ref, g_ref, lse_ref, delta_ref, dq_ref, dk_ref, dv_ref,
    wide, send_kv, send_qg, kv_buf, qg_buf, stats, halo, halo_grad, halo_in, acc,
    dq_buf, dkv_buf, fin_dq, fin_dkv, xq, xl, xacc, xdq, xd_in,
    s_kv, r_kv, s_qg, r_qg, s_st, r_st, s_hf, r_hf, s_hb, r_hb,
    s_dq, r_dq, s_dkv, r_dkv, s_xq, r_xq, s_xl, r_xl, s_xd, r_xd,
):
    rows, heads, dim = q_ref.shape
    hpg = heads // GROUP
    half = 2 * rows
    last = rows_total - 1
    scale = dim ** -0.5
    log2e = math.log2(math.e)

    s, h = lax.axis_index("seq"), lax.axis_index("head")
    lo, m = s % 2, s // 2
    hi, core = h // 2, h % 2
    place = lo * 4 + hi * 2 + core
    mine = hi * 4 + core * 2 + lo

    def peer(o):
        lo2, hi2, core2 = (lo + o % 2) % 2, (hi + o // 2 % 2) % 2, (core + o // 4) % 2
        return (2 * m + lo2, hi2 * 2 + core2), lo2 * 4 + hi2 * 2 + core2, hi2 * 4 + core2 * 2 + lo2

    peers = [(o, *peer(o)) for o in (2, 6, 3, 7, 1, 5, 4)]

    def row(step):
        return (2 * ((m + step + rows_total) % rows_total) + lo, h)

    def copy(src, dst, send, recv, to):
        return pltpu.make_async_remote_copy(
            src_ref=src, dst_ref=dst, send_sem=send, recv_sem=recv, device_id=to, device_id_type=MESH
        )

    def kv_copy(i, o, to, place2, mine2):
        return copy(send_kv.at[mine2, i], kv_buf.at[i, place], s_kv.at[i, o - 1], r_kv.at[i, o - 1], to)

    def qg_copy(i, o, to, place2, mine2):
        return copy(send_qg.at[mine2, i], qg_buf.at[i, place], s_qg.at[i, o - 1], r_qg.at[i, o - 1], to)

    def dq_copy(i, o, to, place2, mine2):
        return copy(dq_buf.at[i, place2], fin_dq.at[mine, i], s_dq.at[i, o - 1], r_dq.at[i, o - 1], to)

    def dkv_copy(i, o, to, place2, mine2):
        return copy(dkv_buf.at[i, place2], fin_dkv.at[mine, i], s_dkv.at[i, o - 1], r_dkv.at[i, o - 1], to)

    def stat_copy():
        return copy(stats.at[lo], stats.at[lo], s_st.at[0], r_st.at[0], peers[4][1])

    def halo_copy(i, n):
        first_half = kv_buf.at[i, pl.ds((4, 0, 4)[n], 2)]
        return copy(first_half, halo.at[i, n], s_hf.at[i, n], r_hf.at[i, n], row((2, 1, 1)[n]))

    def back_copy(i, n):
        return copy(halo_grad.at[i, n], halo_in.at[i, n], s_hb.at[i, n], r_hb.at[i, n], row((-2, -1, -1)[n]))

    def xq_copy(i, n):
        second_half = qg_buf.at[i, pl.ds((2, 2, 6)[n], 2)]
        slot = (2 * (m % 2), 0, 1)[n]
        return copy(second_half, xq.at[i, slot], s_xq.at[i, n], r_xq.at[i, slot], row((-2, -1, -1)[n]))

    def xq_arrived(i, slot):
        to = xq.at[i, slot]
        return copy(to, to, s_xq.at[i, 0], r_xq.at[i, slot], row(1))

    def xl_copy(n):
        slot = (m % 2, 0)[n]
        return copy(stats, xl.at[slot], s_xl.at[n], r_xl.at[slot], row((-2, -1)[n]))

    def xl_arrived(slot):
        return copy(xl.at[slot], xl.at[slot], s_xl.at[0], r_xl.at[slot], row(1))

    def xd_copy(i, n):
        slot = (0, 1, 2 * ((m - (rows_total - 2)) % 2))[n]
        return copy(xdq.at[i, slot], xd_in.at[i, n], s_xd.at[i, n], r_xd.at[i, n], row((1, 1, 2)[n]))

    barrier = pltpu.get_barrier_semaphore()
    for _, to, _, _ in peers:
        pl.semaphore_signal(barrier, inc=1, device_id=to, device_id_type=MESH)
    for step in (1, -1, 2, -2):
        pl.semaphore_signal(barrier, inc=1, device_id=row(step), device_id_type=MESH)

    def split_heads(src, dst, which):
        wide[...] = src[...].astype(F32).reshape(rows * heads, dim)
        for head in range(heads):
            dst[head // hpg, head % hpg, which] = wide[pl.ds(head, rows, stride=heads), :].astype(BF16)

    split_heads(k_ref, send_kv, 0)
    split_heads(v_ref, send_kv, 1)
    kv_buf[:, pl.ds(place, 1)] = send_kv[mine][:, None]
    stats[lo, 0] = lse_ref[...] * log2e
    stats[lo, 1] = delta_ref[...]

    pl.semaphore_wait(barrier, GROUP - 1 + 4)

    stat_copy().start()

    @pl.loop(0, hpg)
    def _(i):
        for p in peers:
            kv_copy(i, *p).start()

    split_heads(q_ref, send_qg, 0)
    split_heads(g_ref, send_qg, 1)
    qg_buf[:, pl.ds(place, 1)] = send_qg[mine][:, None]

    @pl.loop(0, hpg)
    def _(i):
        for p in peers:
            qg_copy(i, *p).start()

    @pl.when(m <= 1)
    def _():
        halo[:, 0] = jnp.zeros_like(halo[:, 0])

    @pl.when(m == 0)
    def _():
        halo[:, 1:3] = jnp.zeros_like(halo[:, 1:3])

    @pl.when(m >= last - 1)
    def _():
        halo_in[:, 0] = jnp.zeros_like(halo_in[:, 0])

    @pl.when(m == last)
    def _():
        halo_in[:, 1:3] = jnp.zeros_like(halo_in[:, 1:3])

    @pl.loop(0, hpg)
    def _(i):
        for p in peers:
            kv_copy(i, *p).wait_recv()

        @pl.when(m <= last - 2)
        def _():
            halo_copy(i, 0).start()

        @pl.when(m <= last - 1)
        def _():
            halo_copy(i, 1).start()
            halo_copy(i, 2).start()

    stat_copy().wait_recv()

    @pl.when(m <= 1)
    def _():
        xl_copy(0).start()

    @pl.when(m == 0)
    def _():
        xl_copy(1).start()

    key_at = lax.broadcasted_iota(jnp.int32, (half, half), 0)
    query_at = lax.broadcasted_iota(jnp.int32, (half, half), 1)
    causal = key_at <= query_at

    def flat(x):
        return x.reshape(-1, dim)

    def tile(kk, vv, qq, gg, lse, delta):
        scores = dot(kk, qq, NT) * (scale * log2e) - lse
        return jnp.exp2(scores), dot(vv, gg, NT) - delta

    def compute(i):
        keys = [halo[i, :, :, 0], kv_buf[i, 0:2, 0], kv_buf[i, 4:6, 0]]
        vals = [halo[i, :, :, 1], kv_buf[i, 0:2, 1], kv_buf[i, 4:6, 1]]
        keys = jnp.concatenate([flat(x) for x in keys], axis=0)
        vals = jnp.concatenate([flat(x) for x in vals], axis=0)
        at = pl.ds(4 * lo + i, 1)
        parts = []
        for b in range(2):
            kk, vv = keys[b * half : (b + 4) * half], vals[b * half : (b + 4) * half]
            k2, v2 = flat(kv_buf[i, 4 * b + 2 : 4 * b + 4, 0]), flat(kv_buf[i, 4 * b + 2 : 4 * b + 4, 1])
            qq, gg = flat(qg_buf[i, 4 * b : 4 * b + 4, 0]), flat(qg_buf[i, 4 * b : 4 * b + 4, 1])
            lse, delta = stats[b, 0, at, :], stats[b, 1, at, :]
            probs, pgrad = tile(kk, vv, qq, gg, lse, delta)
            own = probs[3 * half :]
            own = jnp.concatenate([jnp.where(causal, own[:, :half], 0.0), own[:, half:]], axis=1)
            probs = jnp.concatenate([probs[: 3 * half], own], axis=0)
            sgrad = (probs * pgrad).astype(BF16)
            dv = dot(probs.astype(BF16), gg, NN)
            dk = dot(sgrad, qq, NN) * scale
            q2, g2 = qq[half:], gg[half:]
            probs, pgrad = tile(k2, v2, q2, g2, lse[:, half:], delta[:, half:])
            probs = jnp.where(causal, probs, 0.0)
            sgrad2 = (probs * pgrad).astype(BF16)
            acc[i, b, 1, 1] = dot(probs.astype(BF16), g2, NN)
            acc[i, b, 1, 0] = dot(sgrad2, q2, NN) * scale
            dq = dot(sgrad, kk, TN)
            dq = jnp.concatenate([dq[:half], dq[half:] + dot(sgrad2, k2, TN)], axis=0) * scale
            dq_buf[i, 4 * b : 4 * b + 4] = dq.astype(BF16).reshape(4, rows, dim)
            parts.append((dk, dv))
        for which in range(2):
            e, o = parts[0][which], parts[1][which]
            halo_grad[i, 0, which] = e[:half].astype(BF16)
            halo_grad[i, 1, which] = (e[half : 2 * half] + o[:half]).astype(BF16)
            halo_grad[i, 2, which] = (e[2 * half : 3 * half] + o[half : 2 * half]).astype(BF16)
            acc[i, 0, 0, which] = e[3 * half :] + o[2 * half : 3 * half]
            acc[i, 1, 0, which] = o[3 * half :]

    def wrapped(i, slot, b, first):
        kk, vv = flat(kv_buf[i, 4 * b : 4 * b + 4, 0]), flat(kv_buf[i, 4 * b : 4 * b + 4, 1])
        qq, gg = flat(xq[i, slot, :, 0]), flat(xq[i, slot, :, 1])
        at = pl.ds(4 * lo + i, 1)
        lse = xl[slot // 2, slot % 2, 0, at, :][:, half:]
        delta = xl[slot // 2, slot % 2, 1, at, :][:, half:]
        probs, pgrad = tile(kk, vv, qq, gg, lse, delta)
        sgrad = (probs * pgrad).astype(BF16)
        dv = dot(probs.astype(BF16), gg, NN)
        dk = dot(sgrad, qq, NN) * scale
        for part in range(2):
            cut = slice(part * half, (part + 1) * half)
            acc[i, b, part, 0] += dk[cut]
            acc[i, b, part, 1] += dv[cut]
        dq = dot(sgrad, kk, TN) * scale
        if first:
            xacc[slot] = dq
        else:
            xacc[slot] += dq

    def send_dq(i):
        for p in peers:
            dq_copy(i, *p).start()

    def finish(i):
        @pl.when(m == last)
        def _():
            for slot in range(3):
                xq_arrived(i, slot).wait_recv()
            for slot in range(2):
                wrapped(i, slot, 0, True)
            wrapped(i, 2, 1, True)
            for slot in range(2):
                wrapped(i, slot, 1, False)
            xdq[i] = xacc[...].astype(BF16)
            for n in range(3):
                xd_copy(i, n).start()

        @pl.when(m == last - 1)
        def _():
            xq_arrived(i, 0).wait_recv()
            wrapped(i, 0, 1, True)
            xdq[i, 0] = xacc[0].astype(BF16)
            xd_copy(i, 2).start()

        @pl.when(m <= last - 2)
        def _():
            back_copy(i, 0).wait_recv()

        @pl.when(m <= last - 1)
        def _():
            back_copy(i, 1).wait_recv()
            back_copy(i, 2).wait_recv()

        for which in range(2):
            e = acc[i, 0, 0, which] + halo_in[i, 1, which].astype(F32)
            o = acc[i, 1, 0, which] + halo_in[i, 2, which].astype(F32) + halo_in[i, 0, which].astype(F32)
            for b, first in ((0, e), (1, o)):
                dkv_buf[i, 4 * b : 4 * b + 2, which] = first.astype(BF16).reshape(2, rows, dim)
                second = acc[i, b, 1, which]
                dkv_buf[i, 4 * b + 2 : 4 * b + 4, which] = second.astype(BF16).reshape(2, rows, dim)
        for p in peers:
            dkv_copy(i, *p).start()

        @pl.when(m <= 1)
        def _():
            xd_copy(i, 2).wait_recv()
            more = xd_in[i, 2].astype(F32).reshape(2, rows, dim)
            dq_buf[i, 2:4] = (dq_buf[i, 2:4].astype(F32) + more).astype(BF16)

        @pl.when(m == 0)
        def _():
            for slot in range(2):
                xd_copy(i, slot).wait_recv()
                at = slice(4 * slot + 2, 4 * slot + 4)
                more = xd_in[i, slot].astype(F32).reshape(2, rows, dim)
                dq_buf[i, at] = (dq_buf[i, at].astype(F32) + more).astype(BF16)

        @pl.when(m <= 1)
        def _():
            send_dq(i)

    @pl.when(m == last)
    def _():
        xl_arrived(0).wait_recv()
        xl_arrived(1).wait_recv()

    @pl.when(m == last - 1)
    def _():
        xl_arrived(0).wait_recv()

    @pl.loop(0, hpg)
    def _(i):
        for p in peers:
            qg_copy(i, *p).wait_recv()

        @pl.when(m <= 1)
        def _():
            xq_copy(i, 0).start()

        @pl.when(m == 0)
        def _():
            xq_copy(i, 1).start()
            xq_copy(i, 2).start()

        @pl.when(m >= 2)
        def _():
            halo_copy(i, 0).wait_recv()

        @pl.when(m >= 1)
        def _():
            halo_copy(i, 1).wait_recv()
            halo_copy(i, 2).wait_recv()

        compute(i)

        @pl.when(m >= 2)
        def _():
            back_copy(i, 0).start()

        @pl.when(m >= 1)
        def _():
            back_copy(i, 1).start()
            back_copy(i, 2).start()

        @pl.when(m >= 2)
        def _():
            send_dq(i)

        @pl.when(i >= 1)
        def _():
            finish(i - 1)

    finish(hpg - 1)

    @pl.loop(0, hpg)
    def _(i):
        for p in peers:
            dq_copy(i, *p).wait_recv()
        fin_dq[mine, i] = dq_buf[i, place]

    def join_heads(src, dst):
        for head in range(heads):
            wide[pl.ds(head, rows, stride=heads), :] = src(head // hpg, head % hpg).astype(F32)
        dst[...] = wide[...].reshape(rows, heads, dim).astype(BF16)

    join_heads(lambda j, i: fin_dq[j, i], dq_ref)

    @pl.loop(0, hpg)
    def _(i):
        for p in peers:
            dkv_copy(i, *p).wait_recv()
        fin_dkv[mine, i] = dkv_buf[i, place]

    join_heads(lambda j, i: fin_dkv[j, i, 0], dk_ref)
    join_heads(lambda j, i: fin_dkv[j, i, 1], dv_ref)

    stat_copy().wait_send()

    @pl.loop(0, hpg)
    def _(i):
        for p in peers:
            kv_copy(i, *p).wait_send()
            qg_copy(i, *p).wait_send()
            dq_copy(i, *p).wait_send()
            dkv_copy(i, *p).wait_send()

        @pl.when(m <= last - 2)
        def _():
            halo_copy(i, 0).wait_send()

        @pl.when(m <= last - 1)
        def _():
            halo_copy(i, 1).wait_send()
            halo_copy(i, 2).wait_send()

        @pl.when(m >= 2)
        def _():
            back_copy(i, 0).wait_send()

        @pl.when(m >= 1)
        def _():
            back_copy(i, 1).wait_send()
            back_copy(i, 2).wait_send()

        @pl.when(m <= 1)
        def _():
            xq_copy(i, 0).wait_send()

        @pl.when(m == 0)
        def _():
            xq_copy(i, 1).wait_send()
            xq_copy(i, 2).wait_send()

        @pl.when(m >= last - 1)
        def _():
            xd_copy(i, 2).wait_send()

        @pl.when(m == last)
        def _():
            xd_copy(i, 0).wait_send()
            xd_copy(i, 1).wait_send()

    @pl.when(m <= 1)
    def _():
        xl_copy(0).wait_send()

    @pl.when(m == 0)
    def _():
        xl_copy(1).wait_send()


def on_device(queries, key_vectors, value_vectors, grad_output, logsumexp, row_delta):
    rows, heads, dim = queries.shape
    hpg = heads // GROUP
    half = 2 * rows
    rows_total = lax.axis_size("seq") // 2
    vmem = pl.BlockSpec(memory_space=pltpu.VMEM)
    dma = pltpu.SemaphoreType.DMA
    out = jax.ShapeDtypeStruct((rows, heads, dim), BF16)

    def body(*refs):
        kernel(rows_total, *refs)

    return pl.pallas_call(
        body,
        out_shape=(out, out, out),
        in_specs=[vmem] * 6,
        out_specs=(vmem, vmem, vmem),
        scratch_shapes=[
            pltpu.VMEM((rows * heads, dim), F32),
            pltpu.VMEM((GROUP, hpg, 2, rows, dim), BF16),
            pltpu.VMEM((GROUP, hpg, 2, rows, dim), BF16),
            pltpu.VMEM((hpg, GROUP, 2, rows, dim), BF16),
            pltpu.VMEM((hpg, GROUP, 2, rows, dim), BF16),
            pltpu.VMEM((2, 2, *logsumexp.shape), F32),
            pltpu.VMEM((hpg, 3, 2, 2, rows, dim), BF16),
            pltpu.VMEM((hpg, 3, 2, half, dim), BF16),
            pltpu.VMEM((hpg, 3, 2, half, dim), BF16),
            pltpu.VMEM((hpg, 2, 2, 2, half, dim), F32),
            pltpu.VMEM((hpg, GROUP, rows, dim), BF16),
            pltpu.VMEM((hpg, GROUP, 2, rows, dim), BF16),
            pltpu.VMEM((GROUP, hpg, rows, dim), BF16),
            pltpu.VMEM((GROUP, hpg, 2, rows, dim), BF16),
            pltpu.VMEM((hpg, 3, 2, 2, rows, dim), BF16),
            pltpu.VMEM((2, 2, 2, *logsumexp.shape), F32),
            pltpu.VMEM((3, half, dim), F32),
            pltpu.VMEM((hpg, 3, half, dim), BF16),
            pltpu.VMEM((hpg, 3, half, dim), BF16),
            *[dma((hpg, GROUP - 1))] * 4,
            *[dma((1,))] * 2,
            *[dma((hpg, 3))] * 4,
            *[dma((hpg, GROUP - 1))] * 4,
            *[dma((hpg, 3))] * 2,
            *[dma((2,))] * 2,
            *[dma((hpg, 3))] * 2,
        ],
        compiler_params=pltpu.CompilerParams(
            collective_id=0, has_side_effects=True, vmem_limit_bytes=48 << 20
        ),
        name="window_grads",
    )(queries, key_vectors, value_vectors, grad_output, logsumexp, row_delta)


def solution(mesh):
    rows = P(("seq", "head"), None, None)
    stats = P("head", "seq")
    return jax.shard_map(
        on_device,
        mesh=mesh,
        in_specs=(rows, rows, rows, rows, stats, stats),
        out_specs=(rows, rows, rows),
        check_vma=False,
    )
```

time: 263 us -> 88.6 us (0.34)
  waiting for transfers between devices: 150 us -> 0 us
  Pallas kernels: 0 us -> 79.7 us
  starting transfers between devices: 79.6 us -> 0 us
  matrix products: 19.4 us -> 0 us
  local copies, waits for them, and re-layouts: 12.2 us -> 7.93 us
    ppermute x12 -> x0, waiting for transfers between devices: 87.3 us -> none  [shifted(): return lax.ppermute(block, axis, route)]
    pallas_call x0 -> x1, Pallas kernels: none -> 79.7 us  [on_device(): pl.pallas_call(body, out_shape=(out, out, out), in_specs=[vmem] * 6, out_...]
    all_to_all x7 -> x0, waiting for transfers between devices: 62.5 us -> none  [the longest x1 14.6 us: on_device(): lax.all_to_all(q_final, 'head', split_axis=0, concat_axis=1, tiled=True)]
    ppermute x12 -> x0, starting transfers between devices: 41.4 us -> none  [shifted(): return lax.ppermute(block, axis, route)]
    all_to_all x7 -> x0, starting transfers between devices: 38.2 us -> none  [the longest x1 10.3 us: on_device(): lax.all_to_all(queries, 'head', split_axis=1, concat_axis=0, tiled=True)]
    dot_general x20 -> x0, matrix products: 19.4 us -> none  [the longest x4 5.66 us: tile_grads(): jnp.einsum('hqk,qhd->khd', probs.astype(jnp.bfloat16), g_rows, preferred_...]
    all_to_all x7 -> x0, local copies, waits for them, and re-layouts: 3.59 us -> none  [the longest x1 0.88 us: on_device(): lax.all_to_all(k_final, 'head', split_axis=0, concat_axis=1, tiled=True)]
    convert_element_type x3 -> x0, local copies, waits for them, and re-layouts: 3.41 us -> none  [the longest x1 1.14 us: on_device(): v_final = v_total.astype(jnp.bfloat16)]
  transfers between devices with their start and end apart: 19 -> 0, of which waited for: 13 -> 0; matrix products, arithmetic and copies ran while one was open for 10% -> 0% of each run, Pallas kernels for 0% -> 0%
where the time goes in v1:
time: 88.6 us; the launch traced here: 88.2 us
  Pallas kernels  79.7 us (90%)
  local copies, waits for them, and re-layouts  7.93 us (9%)
    pallas_call x1, Pallas kernels, on_device(): pl.pallas_call(body, out_shape=(out, out, out), in_specs=[vmem] * 6, out_...  79.7 us
    unnamed x15, local copies, waits for them, and re-layouts  7.93 us

profile of v1, /device:TPU:1, one launch (start us, length us, event | category | flops | bytes accessed | tf_op | source)
XLA Modules:
  0.0 88.2 jit_solution(697508587311594015)
XLA Ops:
  0.6 0.0 copy-start
  0.6 1.0 %copy-done = bf16[64,32,128]{2,1,0:T(8,128)(2,1)S(1)} copy-done((bf16[64,32,128]{2,1,0:T(8,128)(2,1)S(1)}, bf16[64,32,128]{2,1,0:T(8,128)(2,1)}, u32[]{:S(2)}) %copy-start) | copy-done | bytes 524312
  1.7 0.0 copy-start.1
  1.7 1.0 %copy-done.1 = bf16[64,32,128]{2,1,0:T(8,128)(2,1)S(1)} copy-done((bf16[64,32,128]{2,1,0:T(8,128)(2,1)S(1)}, bf16[64,32,128]{2,1,0:T(8,128)(2,1)}, u32[]{:S(2)}) %copy-start.1) | copy-done | bytes 524312
  2.7 0.0 copy-start.2
  2.7 1.0 %copy-done.2 = bf16[64,32,128]{2,1,0:T(8,128)(2,1)S(1)} copy-done((bf16[64,32,128]{2,1,0:T(8,128)(2,1)S(1)}, bf16[64,32,128]{2,1,0:T(8,128)(2,1)}, u32[]{:S(2)}) %copy-start.2) | copy-done | bytes 524312
  3.8 0.0 copy-start.3
  3.8 1.0 %copy-done.3 = bf16[64,32,128]{2,1,0:T(8,128)(2,1)S(1)} copy-done((bf16[64,32,128]{2,1,0:T(8,128)(2,1)S(1)}, bf16[64,32,128]{2,1,0:T(8,128)(2,1)}, u32[]{:S(2)}) %copy-start.3) | copy-done | bytes 524312
  4.8 0.0 copy-start.4
  4.8 0.7 copy-done.4
  5.5 0.0 copy-start.5
  5.5 0.7 copy-done.5
  6.2 79.7 %window_grads.1 = (bf16[64,32,128]{2,1,0:T(8,128)(2,1)S(1)}, bf16[64,32,128]{2,1,0:T(8,128)(2,1)S(1)}, bf16[64,32,128]{2,1,0:T(8,128)(2,1)S(1)}) custom-call(bf16[64,32,128]{2,1,0:T(8,128)(2,1)S(1)} %copy-done, bf16[64,32,128]{2,1,0:T(8,128)(2,1)S(1)} %copy-done.1, bf16[64,32,128]{2,1,0:T(8,128)(2,1)S(1)} %copy-done.2, bf16[64,32,128]{2,1,0:T(8,128)(2,1)S(1)} %copy-done.3, ...), custom_call_target="tpu_custom_call" | custom-call | tf_op jit(solution)/shard_map/window_grads/pallas_call | solution.py:445
  85.9 0.8 copy.12
  86.7 0.8 copy.13
  87.5 0.8 copy.14
Async XLA Ops:
  0.6 1.0 %copy-start = (bf16[64,32,128]{2,1,0:T(8,128)(2,1)S(1)}, bf16[64,32,128]{2,1,0:T(8,128)(2,1)}, u32[]{:S(2)}) copy-start(bf16[64,32,128]{2,1,0:T(8,128)(2,1)} %refs_0_.1) | copy-start | bytes 1572868
  1.7 1.0 %copy-start.1 = (bf16[64,32,128]{2,1,0:T(8,128)(2,1)S(1)}, bf16[64,32,128]{2,1,0:T(8,128)(2,1)}, u32[]{:S(2)}) copy-start(bf16[64,32,128]{2,1,0:T(8,128)(2,1)} %refs_1_.1) | copy-start | bytes 1572868
  2.7 1.0 %copy-start.2 = (bf16[64,32,128]{2,1,0:T(8,128)(2,1)S(1)}, bf16[64,32,128]{2,1,0:T(8,128)(2,1)}, u32[]{:S(2)}) copy-start(bf16[64,32,128]{2,1,0:T(8,128)(2,1)} %refs_2_.1) | copy-start | bytes 1572868
  3.8 1.0 %copy-start.3 = (bf16[64,32,128]{2,1,0:T(8,128)(2,1)S(1)}, bf16[64,32,128]{2,1,0:T(8,128)(2,1)}, u32[]{:S(2)}) copy-start(bf16[64,32,128]{2,1,0:T(8,128)(2,1)} %refs_3_.1) | copy-start | bytes 1572868
  4.8 0.7 copy-start.4
  5.5 0.7 copy-start.5

commit v2 on v1

--- a/solution.py
+++ b/solution.py
@@ -20,9 +20,9 @@
 
 
 def kernel(
-    rows_total, q_ref, k_ref, v_ref, g_ref, lse_ref, delta_ref, dq_ref, dk_ref, dv_ref,
-    wide, send_kv, send_qg, kv_buf, qg_buf, stats, halo, halo_grad, halo_in, acc,
-    dq_buf, dkv_buf, fin_dq, fin_dkv, xq, xl, xacc, xdq, xd_in,
+    rows_total, q_ref, k_ref, v_ref, g_ref, lse_ref, delta_ref, fin_dq, fin_dkv,
+    send_kv, send_qg, kv_buf, qg_buf, stats, halo, halo_grad, halo_in, acc,
+    dq_buf, dkv_buf, xq, xl, xacc, xdq, xd_in, chain, local, local_stats, ready, s_in, s_own,
     s_kv, r_kv, s_qg, r_qg, s_st, r_st, s_hf, r_hf, s_hb, r_hb,
     s_dq, r_dq, s_dkv, r_dkv, s_xq, r_xq, s_xl, r_xl, s_xd, r_xd,
 ):
@@ -65,20 +65,28 @@
     def dkv_copy(i, o, to, place2, mine2):
         return copy(dkv_buf.at[i, place2], fin_dkv.at[mine, i], s_dkv.at[i, o - 1], r_dkv.at[i, o - 1], to)
 
+    def keep(i):
+        return (
+            pltpu.make_async_copy(dq_buf.at[i, place], fin_dq.at[mine, i], s_own.at[i, 0]),
+            pltpu.make_async_copy(dkv_buf.at[i, place], fin_dkv.at[mine, i], s_own.at[i, 1]),
+        )
+
     def stat_copy():
         return copy(stats.at[lo], stats.at[lo], s_st.at[0], r_st.at[0], peers[4][1])
 
     def halo_copy(i, n):
-        first_half = kv_buf.at[i, pl.ds((4, 0, 4)[n], 2)]
-        return copy(first_half, halo.at[i, n], s_hf.at[i, n], r_hf.at[i, n], row((2, 1, 1)[n]))
+        src = halo.at[i, 2] if n == 0 else kv_buf.at[i, pl.ds((0, 4)[n - 1], 2)]
+        return copy(src, halo.at[i, n], s_hf.at[i, n], r_hf.at[i, n], row(1))
 
     def back_copy(i, n):
-        return copy(halo_grad.at[i, n], halo_in.at[i, n], s_hb.at[i, n], r_hb.at[i, n], row((-2, -1, -1)[n]))
-
-    def xq_copy(i, n):
-        second_half = qg_buf.at[i, pl.ds((2, 2, 6)[n], 2)]
-        slot = (2 * (m % 2), 0, 1)[n]
-        return copy(second_half, xq.at[i, slot], s_xq.at[i, n], r_xq.at[i, slot], row((-2, -1, -1)[n]))
+        return copy(halo_grad.at[i, n], halo_in.at[i, n], s_hb.at[i, n], r_hb.at[i, n], row(-1))
+
+    def xq_copy(i, slot):
+        second_half = qg_buf.at[i, pl.ds((2, 6, 2)[slot], 2)]
+        return copy(second_half, xq.at[i, slot], s_xq.at[i, slot], r_xq.at[i, slot], row((-1, -1, -2)[slot]))
+
+    def xq_hand_on(i):
+        return copy(xq.at[i, 0], xq.at[i, 0], s_xq.at[i, 0], r_xq.at[i, 0], row(-1))
 
     def xq_arrived(i, slot):
         to = xq.at[i, slot]
@@ -95,40 +103,82 @@
         slot = (0, 1, 2 * ((m - (rows_total - 2)) % 2))[n]
         return copy(xdq.at[i, slot], xd_in.at[i, n], s_xd.at[i, n], r_xd.at[i, n], row((1, 1, 2)[n]))
 
+    loads = [pltpu.make_async_copy(src, local.at[n], s_in.at[n]) for n, src in enumerate((k_ref, v_ref, q_ref, g_ref))]
+    stat_loads = [
+        pltpu.make_async_copy(src, local_stats.at[n], s_in.at[4 + n]) for n, src in enumerate((lse_ref, delta_ref))
+    ]
+    for load in loads[:2] + stat_loads + loads[2:]:
+        load.start()
+
     barrier = pltpu.get_barrier_semaphore()
     for _, to, _, _ in peers:
         pl.semaphore_signal(barrier, inc=1, device_id=to, device_id_type=MESH)
-    for step in (1, -1, 2, -2):
-        pl.semaphore_signal(barrier, inc=1, device_id=row(step), device_id_type=MESH)
-
-    def split_heads(src, dst, which):
-        wide[...] = src[...].astype(F32).reshape(rows * heads, dim)
-        for head in range(heads):
-            dst[head // hpg, head % hpg, which] = wide[pl.ds(head, rows, stride=heads), :].astype(BF16)
-
-    split_heads(k_ref, send_kv, 0)
-    split_heads(v_ref, send_kv, 1)
+
+    def tell(sem, step):
+        pl.semaphore_signal(sem, inc=1, device_id=row(step), device_id_type=MESH)
+
+    @pl.when(m <= last - 1)
+    def _():
+        tell(barrier, 1)
+
+    @pl.when(m >= 1)
+    def _():
+        tell(barrier, -1)
+
+    @pl.when(m <= 1)
+    def _():
+        tell(barrier, -2)
+
+    @pl.when(m == 0)
+    def _():
+        tell(barrier, -1)
+
+    def split_heads(n, dst, which):
+        loads[n].wait()
+        dst[:, :, which] = jnp.swapaxes(local[n], 0, 1).reshape(GROUP, hpg, rows, dim)
+
+    split_heads(0, send_kv, 0)
+    split_heads(1, send_kv, 1)
     kv_buf[:, pl.ds(place, 1)] = send_kv[mine][:, None]
-    stats[lo, 0] = lse_ref[...] * log2e
-    stats[lo, 1] = delta_ref[...]
-
-    pl.semaphore_wait(barrier, GROUP - 1 + 4)
+    for load in stat_loads:
+        load.wait()
+    stats[lo, 0] = local_stats[0] * log2e
+    stats[lo, 1] = local_stats[1]
+
+    one, none = jnp.int32(1), jnp.int32(0)
+    along = jnp.where(m >= 1, one, none) + jnp.where(m <= last - 1, one, none)
+    ends = jnp.where(m >= last - 1, one, none) + jnp.where(m == last, one, none)
+    pl.semaphore_wait(barrier, GROUP - 1 + along + ends)
+
+    @pl.when(m >= last - 1)
+    def _():
+        tell(ready, 2)
+
+    @pl.when(m == last)
+    def _():
+        tell(ready, 1)
 
     stat_copy().start()
 
-    @pl.loop(0, hpg)
-    def _(i):
-        for p in peers:
-            kv_copy(i, *p).start()
-
-    split_heads(q_ref, send_qg, 0)
-    split_heads(g_ref, send_qg, 1)
+    def send(what, first, count):
+        @pl.loop(first, first + count)
+        def _(i):
+            for p in peers:
+                what(i, *p).start()
+
+    send(kv_copy, 0, 2)
+    split_heads(2, send_qg, 0)
+    split_heads(3, send_qg, 1)
     qg_buf[:, pl.ds(place, 1)] = send_qg[mine][:, None]
 
-    @pl.loop(0, hpg)
+    @pl.loop(0, hpg - 2)
     def _(i):
         for p in peers:
             qg_copy(i, *p).start()
+        for p in peers:
+            kv_copy(i + 2, *p).start()
+
+    send(qg_copy, hpg - 2, 2)
 
     @pl.when(m <= 1)
     def _():
@@ -138,32 +188,41 @@
     def _():
         halo[:, 1:3] = jnp.zeros_like(halo[:, 1:3])
 
-    @pl.when(m >= last - 1)
-    def _():
-        halo_in[:, 0] = jnp.zeros_like(halo_in[:, 0])
-
     @pl.when(m == last)
     def _():
-        halo_in[:, 1:3] = jnp.zeros_like(halo_in[:, 1:3])
-
-    @pl.loop(0, hpg)
-    def _(i):
+        halo_in[...] = jnp.zeros_like(halo_in)
+
+    def hand_on(i):
+        @pl.when(m >= 1)
+        def _():
+            halo_copy(i, 2).wait_recv()
+
+            @pl.when(m <= last - 1)
+            def _():
+                halo_copy(i, 0).start()
+
+    def share_keys(i):
         for p in peers:
             kv_copy(i, *p).wait_recv()
 
-        @pl.when(m <= last - 2)
-        def _():
-            halo_copy(i, 0).start()
-
         @pl.when(m <= last - 1)
         def _():
+            halo_copy(i, 2).start()
             halo_copy(i, 1).start()
-            halo_copy(i, 2).start()
+
+    @pl.loop(0, 2)
+    def _(i):
+        share_keys(i)
+
+    @pl.loop(0, 2)
+    def _(i):
+        hand_on(i)
 
     stat_copy().wait_recv()
 
     @pl.when(m <= 1)
     def _():
+        pl.semaphore_wait(ready, 2 - m)
         xl_copy(0).start()
 
     @pl.when(m == 0)
@@ -214,7 +273,7 @@
             e, o = parts[0][which], parts[1][which]
             halo_grad[i, 0, which] = e[:half].astype(BF16)
             halo_grad[i, 1, which] = (e[half : 2 * half] + o[:half]).astype(BF16)
-            halo_grad[i, 2, which] = (e[2 * half : 3 * half] + o[half : 2 * half]).astype(BF16)
+            chain[i, which] = e[2 * half : 3 * half] + o[half : 2 * half]
             acc[i, 0, 0, which] = e[3 * half :] + o[2 * half : 3 * half]
             acc[i, 1, 0, which] = o[3 * half :]
 
@@ -242,11 +301,21 @@
         for p in peers:
             dq_copy(i, *p).start()
 
-    def finish(i):
+    def pass_back(i):
+        @pl.when(m >= 1)
+        def _():
+            @pl.when(m <= last - 1)
+            def _():
+                back_copy(i, 0).wait_recv()
+
+            halo_grad[i, 2] = (chain[i] + halo_in[i, 0].astype(F32)).astype(BF16)
+            back_copy(i, 2).start()
+
+    def wrapped_pairs(i):
         @pl.when(m == last)
         def _():
-            for slot in range(3):
-                xq_arrived(i, slot).wait_recv()
+            xq_arrived(i, 1).wait_recv()
+            xq_arrived(i, 2).wait_recv()
             for slot in range(2):
                 wrapped(i, slot, 0, True)
             wrapped(i, 2, 1, True)
@@ -263,30 +332,25 @@
             xdq[i, 0] = xacc[0].astype(BF16)
             xd_copy(i, 2).start()
 
-        @pl.when(m <= last - 2)
-        def _():
-            back_copy(i, 0).wait_recv()
-
+    def finish(i):
         @pl.when(m <= last - 1)
         def _():
             back_copy(i, 1).wait_recv()
             back_copy(i, 2).wait_recv()
 
         for which in range(2):
-            e = acc[i, 0, 0, which] + halo_in[i, 1, which].astype(F32)
-            o = acc[i, 1, 0, which] + halo_in[i, 2, which].astype(F32) + halo_in[i, 0, which].astype(F32)
-            for b, first in ((0, e), (1, o)):
+            for b in range(2):
+                first = acc[i, b, 0, which] + halo_in[i, 1 + b, which].astype(F32)
                 dkv_buf[i, 4 * b : 4 * b + 2, which] = first.astype(BF16).reshape(2, rows, dim)
                 second = acc[i, b, 1, which]
                 dkv_buf[i, 4 * b + 2 : 4 * b + 4, which] = second.astype(BF16).reshape(2, rows, dim)
         for p in peers:
             dkv_copy(i, *p).start()
 
-        @pl.when(m <= 1)
-        def _():
-            xd_copy(i, 2).wait_recv()
-            more = xd_in[i, 2].astype(F32).reshape(2, rows, dim)
-            dq_buf[i, 2:4] = (dq_buf[i, 2:4].astype(F32) + more).astype(BF16)
+    def finish_first(i):
+        xd_copy(i, 2).wait_recv()
+        more = xd_in[i, 2].astype(F32).reshape(2, rows, dim)
+        dq_buf[i, 2:4] = (dq_buf[i, 2:4].astype(F32) + more).astype(BF16)
 
         @pl.when(m == 0)
         def _():
@@ -296,9 +360,7 @@
                 more = xd_in[i, slot].astype(F32).reshape(2, rows, dim)
                 dq_buf[i, at] = (dq_buf[i, at].astype(F32) + more).astype(BF16)
 
-        @pl.when(m <= 1)
-        def _():
-            send_dq(i)
+        send_dq(i)
 
     @pl.when(m == last)
     def _():
@@ -309,71 +371,99 @@
     def _():
         xl_arrived(0).wait_recv()
 
+    def grads(i):
+        for p in peers:
+            qg_copy(i, *p).wait_recv()
+
+        @pl.when(m == 0)
+        def _():
+            xq_copy(i, 0).start()
+            xq_copy(i, 1).start()
+
+        @pl.when(m == 1)
+        def _():
+            xq_copy(i, 2).start()
+
+        @pl.when(m >= 2)
+        def _():
+            halo_copy(i, 0).wait_recv()
+
+        @pl.when(m >= 1)
+        def _():
+            halo_copy(i, 1).wait_recv()
+
+        compute(i)
+
+        @pl.when(m >= 2)
+        def _():
+            back_copy(i, 0).start()
+
+        @pl.when(m >= 1)
+        def _():
+            back_copy(i, 1).start()
+
+        @pl.when(m >= 2)
+        def _():
+            send_dq(i)
+
     @pl.loop(0, hpg)
     def _(i):
-        for p in peers:
-            qg_copy(i, *p).wait_recv()
-
-        @pl.when(m <= 1)
-        def _():
-            xq_copy(i, 0).start()
-
-        @pl.when(m == 0)
-        def _():
-            xq_copy(i, 1).start()
-            xq_copy(i, 2).start()
-
-        @pl.when(m >= 2)
-        def _():
-            halo_copy(i, 0).wait_recv()
-
-        @pl.when(m >= 1)
-        def _():
-            halo_copy(i, 1).wait_recv()
-            halo_copy(i, 2).wait_recv()
-
-        compute(i)
-
-        @pl.when(m >= 2)
-        def _():
-            back_copy(i, 0).start()
-
-        @pl.when(m >= 1)
-        def _():
-            back_copy(i, 1).start()
-            back_copy(i, 2).start()
-
-        @pl.when(m >= 2)
-        def _():
-            send_dq(i)
+        @pl.when(m == last)
+        def _():
+            xq_arrived(i, 0).wait_recv()
+            xq_hand_on(i).start()
+
+        grads(i)
+
+        @pl.when((i >= 1) & (i + 1 < hpg))
+        def _():
+            hand_on(i + 1)
 
         @pl.when(i >= 1)
         def _():
-            finish(i - 1)
-
-    finish(hpg - 1)
+            pass_back(i - 1)
+
+        @pl.when(i + 2 < hpg)
+        def _():
+            share_keys(i + 2)
+
+        @pl.when(i >= 1)
+        def _():
+            wrapped_pairs(i - 1)
 
     @pl.loop(0, hpg)
     def _(i):
+        finish(i)
+
+        @pl.when(i == 1)
+        def _():
+            pass_back(hpg - 1)
+            wrapped_pairs(hpg - 1)
+
+        @pl.when((m <= 1) & (i >= 2))
+        def _():
+            finish_first(i - 2)
+
+    @pl.when(m <= 1)
+    def _():
+        @pl.loop(hpg - 2, hpg)
+        def _(i):
+            finish_first(i)
+
+    @pl.loop(0, hpg)
+    def _(i):
+        own_dq, own_dkv = keep(i)
+        own_dq.start()
+        own_dkv.start()
+
+    @pl.loop(0, hpg)
+    def _(i):
         for p in peers:
             dq_copy(i, *p).wait_recv()
-        fin_dq[mine, i] = dq_buf[i, place]
-
-    def join_heads(src, dst):
-        for head in range(heads):
-            wide[pl.ds(head, rows, stride=heads), :] = src(head // hpg, head % hpg).astype(F32)
-        dst[...] = wide[...].reshape(rows, heads, dim).astype(BF16)
-
-    join_heads(lambda j, i: fin_dq[j, i], dq_ref)
-
-    @pl.loop(0, hpg)
-    def _(i):
-        for p in peers:
             dkv_copy(i, *p).wait_recv()
-        fin_dkv[mine, i] = dkv_buf[i, place]
-
-    join_heads(lambda j, i: fin_dkv[j, i, 0], dk_ref)
-    join_heads(lambda j, i: fin_dkv[j, i, 1], dv_ref)
+        own_dq, own_dkv = keep(i)
+        own_dq.wait()
+        own_dkv.wait()
 
     stat_copy().wait_send()
 
@@ -385,15 +475,15 @@
             dq_copy(i, *p).wait_send()
             dkv_copy(i, *p).wait_send()
 
-        @pl.when(m <= last - 2)
-        def _():
-            halo_copy(i, 0).wait_send()
-
         @pl.when(m <= last - 1)
         def _():
             halo_copy(i, 1).wait_send()
             halo_copy(i, 2).wait_send()
 
+            @pl.when(m >= 1)
+            def _():
+                halo_copy(i, 0).wait_send()
+
         @pl.when(m >= 2)
         def _():
             back_copy(i, 0).wait_send()
@@ -403,14 +493,18 @@
             back_copy(i, 1).wait_send()
             back_copy(i, 2).wait_send()
 
-        @pl.when(m <= 1)
+        @pl.when(m == 0)
         def _():
             xq_copy(i, 0).wait_send()
-
-        @pl.when(m == 0)
-        def _():
             xq_copy(i, 1).wait_send()
+
+        @pl.when(m == 1)
+        def _():
             xq_copy(i, 2).wait_send()
+
+        @pl.when(m == last)
+        def _():
+            xq_hand_on(i).wait_send()
 
         @pl.when(m >= last - 1)
         def _():
@@ -435,20 +529,20 @@
     hpg = heads // GROUP
     half = 2 * rows
     rows_total = lax.axis_size("seq") // 2
-    vmem = pl.BlockSpec(memory_space=pltpu.VMEM)
+    hbm = pl.BlockSpec(memory_space=pl.ANY)
     dma = pltpu.SemaphoreType.DMA
-    out = jax.ShapeDtypeStruct((rows, heads, dim), BF16)
+    dq_shape = jax.ShapeDtypeStruct((GROUP, hpg, rows, dim), BF16)
+    dkv_shape = jax.ShapeDtypeStruct((GROUP, hpg, 2, rows, dim), BF16)
 
     def body(*refs):
         kernel(rows_total, *refs)
 
-    return pl.pallas_call(
+    dq, dkv = pl.pallas_call(
         body,
-        out_shape=(out, out, out),
-        in_specs=[vmem] * 6,
-        out_specs=(vmem, vmem, vmem),
+        out_shape=(dq_shape, dkv_shape),
+        in_specs=[hbm] * 6,
+        out_specs=(hbm, hbm),
         scratch_shapes=[
-            pltpu.VMEM((rows * heads, dim), F32),
             pltpu.VMEM((GROUP, hpg, 2, rows, dim), BF16),
             pltpu.VMEM((GROUP, hpg, 2, rows, dim), BF16),
             pltpu.VMEM((hpg, GROUP, 2, rows, dim), BF16),
@@ -460,13 +554,17 @@
             pltpu.VMEM((hpg, 2, 2, 2, half, dim), F32),
             pltpu.VMEM((hpg, GROUP, rows, dim), BF16),
             pltpu.VMEM((hpg, GROUP, 2, rows, dim), BF16),
-            pltpu.VMEM((GROUP, hpg, rows, dim), BF16),
-            pltpu.VMEM((GROUP, hpg, 2, rows, dim), BF16),
             pltpu.VMEM((hpg, 3, 2, 2, rows, dim), BF16),
             pltpu.VMEM((2, 2, 2, *logsumexp.shape), F32),
             pltpu.VMEM((3, half, dim), F32),
             pltpu.VMEM((hpg, 3, half, dim), BF16),
             pltpu.VMEM((hpg, 3, half, dim), BF16),
+            pltpu.VMEM((hpg, 2, half, dim), F32),
+            pltpu.VMEM((4, rows, heads, dim), BF16),
+            pltpu.VMEM((2, *logsumexp.shape), F32),
+            pltpu.SemaphoreType.REGULAR,
+            dma((6,)),
+            dma((hpg, 2)),
             *[dma((hpg, GROUP - 1))] * 4,
             *[dma((1,))] * 2,
             *[dma((hpg, 3))] * 4,
@@ -476,10 +574,15 @@
             *[dma((hpg, 3))] * 2,
         ],
         compiler_params=pltpu.CompilerParams(
-            collective_id=0, has_side_effects=True, vmem_limit_bytes=48 << 20
+            collective_id=0, has_side_effects=True, vmem_limit_bytes=60 << 20
         ),
         name="window_grads",
     )(queries, key_vectors, value_vectors, grad_output, logsumexp, row_delta)
+
+    def by_row(x):
+        return jnp.swapaxes(x.reshape(heads, rows, dim), 0, 1)
+
+    return by_row(dq), by_row(dkv[:, :, 0]), by_row(dkv[:, :, 1])
 
 
 def solution(mesh):

time: 88.6 us -> 66.9 us (0.76)
  Pallas kernels: 79.7 us -> 62.1 us
  local copies, waits for them, and re-layouts: 7.93 us -> 4 us
    pallas_call x1, Pallas kernels: 79.7 us -> 62.1 us  [on_device(): pl.pallas_call(body, out_shape=(dq_shape, dkv_shape), in_specs=[hbm] * 6,...]
    unnamed x15 -> x2, local copies, waits for them, and re-layouts: 7.93 us -> 0.01 us
    reshape x0 -> x1, local copies, waits for them, and re-layouts: none -> 2.26 us  [by_row(): return jnp.swapaxes(x.reshape(heads, rows, dim), 0, 1)]
    transpose x0 -> x1, local copies, waits for them, and re-layouts: none -> 1.64 us  [by_row(): return jnp.swapaxes(x.reshape(heads, rows, dim), 0, 1)]
where the time goes in v2:
time: 66.9 us; the launch traced here: 66.8 us
  Pallas kernels  62.1 us (93%)
  local copies, waits for them, and re-layouts  4 us (6%)
    pallas_call x1, Pallas kernels, on_device(): pl.pallas_call(body, out_shape=(dq_shape, dkv_shape), in_specs=[hbm] * 6,...  62.1 us
    reshape x1, local copies, waits for them, and re-layouts, by_row(): return jnp.swapaxes(x.reshape(heads, rows, dim), 0, 1)  2.26 us
    transpose x1, local copies, waits for them, and re-layouts, by_row(): return jnp.swapaxes(x.reshape(heads, rows, dim), 0, 1)  1.64 us

profile of v2, /device:TPU:1, one launch (start us, length us, event | category | flops | bytes accessed | tf_op | source)
XLA Modules:
  0.0 66.8 jit_solution(18081328604862038899)
XLA Ops:
  0.6 62.1 %window_grads.1 = (bf16[8,4,64,128]{3,2,1,0:T(8,128)(2,1)}, bf16[8,4,2,64,128]{4,3,2,1,0:T(8,128)(2,1)}) custom-call(bf16[64,32,128]{2,1,0:T(8,128)(2,1)} %refs_0_.1, bf16[64,32,128]{2,1,0:T(8,128)(2,1)} %refs_1_.1, bf16[64,32,128]{2,1,0:T(8,128)(2,1)} %refs_2_.1, bf16[64,32,128]{2,1,0:T(8,128)(2,1)} %refs_3_.1, f32[8,256]{1,0:T(8,128)} %refs_4_.1, ...), custom_call_target="tpu_custom_call" | custom-call | tf_op jit(solution)/shard_map/window_grads/pallas_call | solution.py:540
  62.8 0.0 copy-start
  62.8 2.3 %copy.15 = bf16[32,64,128]{2,0,1:T(8,128)(2,1)} copy(bf16[32,64,128]{2,1,0:T(8,128)(2,1)} %bitcast.13) | data formatting | bytes 1048576 | tf_op jit(solution)/shard_map/reshape | solution.py:583
  65.0 0.0 copy-done
  65.0 0.1 fusion
  65.1 1.6 %copy_bitcast_fusion = (bf16[64,32,128]{2,1,0:T(8,128)(2,1)}, bf16[64,32,128]{2,1,0:T(8,128)(2,1)}) fusion(bf16[32,64,128]{2,1,0:T(8,128)(2,1)S(1)} %bitcast.10, bf16[32,64,128]{2,1,0:T(8,128)(2,1)S(1)} %bitcast.11), kind=kLoop, calls=%fused_computation | loop fusion | bytes 2097152 | tf_op jit(solution)/shard_map/transpose | solution.py:583
Async XLA Ops:
  62.8 2.3 %copy-start = (bf16[8,4,2,64,128]{4,3,2,1,0:T(8,128)(2,1)S(1)}, bf16[8,4,2,64,128]{4,3,2,1,0:T(8,128)(2,1)}, u32[]{:S(2)}) copy-start(bf16[8,4,2,64,128]{4,3,2,1,0:T(8,128)(2,1)} %get-tuple-element.6) | copy-start | bytes 3145732

commit v3 on v2

--- a/solution.py
+++ b/solution.py
@@ -21,9 +21,9 @@
 
 def kernel(
     rows_total, q_ref, k_ref, v_ref, g_ref, lse_ref, delta_ref, fin_dq, fin_dkv,
-    send_kv, send_qg, kv_buf, qg_buf, stats, halo, halo_grad, halo_in, acc,
+    sent, got, stats, halo, halo_grad, halo_in, acc,
     dq_buf, dkv_buf, xq, xl, xacc, xdq, xd_in, chain, local, local_stats, ready, s_in, s_own,
-    s_kv, r_kv, s_qg, r_qg, s_st, r_st, s_hf, r_hf, s_hb, r_hb,
+    s_split, r_split, s_st, r_st, s_hf, r_hf, s_hb, r_hb,
     s_dq, r_dq, s_dkv, r_dkv, s_xq, r_xq, s_xl, r_xl, s_xd, r_xd,
 ):
     rows, heads, dim = q_ref.shape
@@ -53,11 +53,25 @@
             src_ref=src, dst_ref=dst, send_sem=send, recv_sem=recv, device_id=to, device_id_type=MESH
         )
 
-    def kv_copy(i, o, to, place2, mine2):
-        return copy(send_kv.at[mine2, i], kv_buf.at[i, place], s_kv.at[i, o - 1], r_kv.at[i, o - 1], to)
-
-    def qg_copy(i, o, to, place2, mine2):
-        return copy(send_qg.at[mine2, i], qg_buf.at[i, place], s_qg.at[i, o - 1], r_qg.at[i, o - 1], to)
+    kv_buf, qg_buf = got.at[0], got.at[1]
+
+    def split_copy(kind, i, o, to, place2, mine2):
+        return copy(
+            sent.at[kind, mine2, i], got.at[kind, i, place], s_split.at[kind, i, o - 1], r_split.at[kind, i, o - 1], to
+        )
+
+    def split_arrived(kind, i, part):
+        @pl.when(hi == part)
+        def _():
+            for p in peers:
+                if p[0] in (1, 4, 5):
+                    split_copy(kind, i, *p).wait_recv()
+
+        @pl.when(hi != part)
+        def _():
+            for p in peers:
+                if p[0] not in (1, 4, 5):
+                    split_copy(kind, i, *p).wait_recv()
 
     def dq_copy(i, o, to, place2, mine2):
         return copy(dq_buf.at[i, place2], fin_dq.at[mine, i], s_dq.at[i, o - 1], r_dq.at[i, o - 1], to)
@@ -81,12 +95,10 @@
     def back_copy(i, n):
         return copy(halo_grad.at[i, n], halo_in.at[i, n], s_hb.at[i, n], r_hb.at[i, n], row(-1))
 
-    def xq_copy(i, slot):
-        second_half = qg_buf.at[i, pl.ds((2, 6, 2)[slot], 2)]
-        return copy(second_half, xq.at[i, slot], s_xq.at[i, slot], r_xq.at[i, slot], row((-1, -1, -2)[slot]))
-
-    def xq_hand_on(i):
-        return copy(xq.at[i, 0], xq.at[i, 0], s_xq.at[i, 0], r_xq.at[i, 0], row(-1))
+    def xq_copy(i, n):
+        second_half = qg_buf.at[i, pl.ds((2, 6, 2)[n], 2)]
+        slot = (0, 1, 2 * (m % 2))[n]
+        return copy(second_half, xq.at[i, slot], s_xq.at[i, n], r_xq.at[i, slot], row((-1, -1, -2)[n]))
 
     def xq_arrived(i, slot):
         to = xq.at[i, slot]
@@ -103,11 +115,15 @@
         slot = (0, 1, 2 * ((m - (rows_total - 2)) % 2))[n]
         return copy(xdq.at[i, slot], xd_in.at[i, n], s_xd.at[i, n], r_xd.at[i, n], row((1, 1, 2)[n]))
 
-    loads = [pltpu.make_async_copy(src, local.at[n], s_in.at[n]) for n, src in enumerate((k_ref, v_ref, q_ref, g_ref))]
+    def load_of(n, src=k_ref):
+        return pltpu.make_async_copy(src, local.at[n], s_in.at[n])
+
     stat_loads = [
         pltpu.make_async_copy(src, local_stats.at[n], s_in.at[4 + n]) for n, src in enumerate((lse_ref, delta_ref))
     ]
-    for load in loads[:2] + stat_loads + loads[2:]:
+    for n, src in enumerate((k_ref, v_ref, q_ref, g_ref)):
+        load_of(n, src).start()
+    for load in stat_loads:
         load.start()
 
     barrier = pltpu.get_barrier_semaphore()
@@ -133,13 +149,15 @@
     def _():
         tell(barrier, -1)
 
-    def split_heads(n, dst, which):
-        loads[n].wait()
-        dst[:, :, which] = jnp.swapaxes(local[n], 0, 1).reshape(GROUP, hpg, rows, dim)
-
-    split_heads(0, send_kv, 0)
-    split_heads(1, send_kv, 1)
-    kv_buf[:, pl.ds(place, 1)] = send_kv[mine][:, None]
+    def split_heads(kind):
+        for which in range(2):
+            load_of(2 * kind + which).wait()
+            by_head = jnp.swapaxes(local[2 * kind + which], 0, 1)
+            sent[kind, :, :, which] = by_head.reshape(GROUP, hpg, rows, dim)
+        got[kind, :, pl.ds(place, 1)] = sent[kind, mine][:, None]
+
+    first, second = hi, 1 - hi
+    split_heads(first)
     for load in stat_loads:
         load.wait()
     stats[lo, 0] = local_stats[0] * log2e
@@ -160,25 +178,26 @@
 
     stat_copy().start()
 
-    def send(what, first, count):
-        @pl.loop(first, first + count)
-        def _(i):
-            for p in peers:
-                what(i, *p).start()
-
-    send(kv_copy, 0, 2)
-    split_heads(2, send_qg, 0)
-    split_heads(3, send_qg, 1)
-    qg_buf[:, pl.ds(place, 1)] = send_qg[mine][:, None]
+    def send(kind, i):
+        for p in peers:
+            split_copy(kind, i, *p).start()
+
+    @pl.loop(0, 2)
+    def _(i):
+        send(first, i)
+
+    split_heads(second)
 
     @pl.loop(0, hpg - 2)
     def _(i):
-        for p in peers:
-            qg_copy(i, *p).start()
-        for p in peers:
-            kv_copy(i + 2, *p).start()
-
-    send(qg_copy, hpg - 2, 2)
+        send(second, i)
+        send(first, i + 2)
+
+    @pl.loop(hpg - 2, hpg)
+    def _(i):
+        send(second, i)
+
+    acc[...] = jnp.zeros_like(acc)
 
     @pl.when(m <= 1)
     def _():
@@ -201,22 +220,24 @@
             def _():
                 halo_copy(i, 0).start()
 
-    def share_keys(i):
-        for p in peers:
-            kv_copy(i, *p).wait_recv()
+    def share(i):
+        split_arrived(0, i, 0)
 
         @pl.when(m <= last - 1)
         def _():
             halo_copy(i, 2).start()
             halo_copy(i, 1).start()
 
-    @pl.loop(0, 2)
-    def _(i):
-        share_keys(i)
-
-    @pl.loop(0, 2)
-    def _(i):
-        hand_on(i)
+        split_arrived(1, i, 1)
+
+        @pl.when(m == 0)
+        def _():
+            xq_copy(i, 0).start()
+            xq_copy(i, 1).start()
+
+        @pl.when(m <= 1)
+        def _():
+            xq_copy(i, 2).start()
 
     stat_copy().wait_recv()
 
@@ -228,6 +249,14 @@
     @pl.when(m == 0)
     def _():
         xl_copy(1).start()
+
+    @pl.loop(0, 2)
+    def _(i):
+        share(i)
+
+    @pl.loop(0, 2)
+    def _(i):
+        hand_on(i)
 
     key_at = lax.broadcasted_iota(jnp.int32, (half, half), 0)
     query_at = lax.broadcasted_iota(jnp.int32, (half, half), 1)
@@ -263,8 +292,8 @@
             probs, pgrad = tile(k2, v2, q2, g2, lse[:, half:], delta[:, half:])
             probs = jnp.where(causal, probs, 0.0)
             sgrad2 = (probs * pgrad).astype(BF16)
-            acc[i, b, 1, 1] = dot(probs.astype(BF16), g2, NN)
-            acc[i, b, 1, 0] = dot(sgrad2, q2, NN) * scale
+            acc[i, b, 1, 1] += dot(probs.astype(BF16), g2, NN)
+            acc[i, b, 1, 0] += dot(sgrad2, q2, NN) * scale
             dq = dot(sgrad, kk, TN)
             dq = jnp.concatenate([dq[:half], dq[half:] + dot(sgrad2, k2, TN)], axis=0) * scale
             dq_buf[i, 4 * b : 4 * b + 4] = dq.astype(BF16).reshape(4, rows, dim)
@@ -274,8 +303,8 @@
             halo_grad[i, 0, which] = e[:half].astype(BF16)
             halo_grad[i, 1, which] = (e[half : 2 * half] + o[:half]).astype(BF16)
             chain[i, which] = e[2 * half : 3 * half] + o[half : 2 * half]
-            acc[i, 0, 0, which] = e[3 * half :] + o[2 * half : 3 * half]
-            acc[i, 1, 0, which] = o[3 * half :]
+            acc[i, 0, 0, which] += e[3 * half :] + o[2 * half : 3 * half]
+            acc[i, 1, 0, which] += o[3 * half :]
 
     def wrapped(i, slot, b, first):
         kk, vv = flat(kv_buf[i, 4 * b : 4 * b + 4, 0]), flat(kv_buf[i, 4 * b : 4 * b + 4, 1])
@@ -311,11 +340,11 @@
             halo_grad[i, 2] = (chain[i] + halo_in[i, 0].astype(F32)).astype(BF16)
             back_copy(i, 2).start()
 
-    def wrapped_pairs(i):
+    def wrapped_last(i):
         @pl.when(m == last)
         def _():
-            xq_arrived(i, 1).wait_recv()
-            xq_arrived(i, 2).wait_recv()
+            for slot in range(3):
+                xq_arrived(i, slot).wait_recv()
             for slot in range(2):
                 wrapped(i, slot, 0, True)
             wrapped(i, 2, 1, True)
@@ -325,6 +354,7 @@
             for n in range(3):
                 xd_copy(i, n).start()
 
+    def wrapped_one(i):
         @pl.when(m == last - 1)
         def _():
             xq_arrived(i, 0).wait_recv()
@@ -372,18 +402,7 @@
         xl_arrived(0).wait_recv()
 
     def grads(i):
-        for p in peers:
-            qg_copy(i, *p).wait_recv()
-
-        @pl.when(m == 0)
-        def _():
-            xq_copy(i, 0).start()
-            xq_copy(i, 1).start()
-
-        @pl.when(m == 1)
-        def _():
-            xq_copy(i, 2).start()
-
+        split_arrived(1, i, 0)
         @pl.when(m >= 2)
         def _():
             halo_copy(i, 0).wait_recv()
@@ -408,11 +427,8 @@
 
     @pl.loop(0, hpg)
     def _(i):
-        @pl.when(m == last)
-        def _():
-            xq_arrived(i, 0).wait_recv()
-            xq_hand_on(i).start()
-
+        split_arrived(0, i, 1)
+        wrapped_last(i)
         grads(i)
 
         @pl.when((i >= 1) & (i + 1 < hpg))
@@ -425,11 +441,13 @@
 
         @pl.when(i + 2 < hpg)
         def _():
-            share_keys(i + 2)
+            share(i + 2)
 
         @pl.when(i >= 1)
         def _():
-            wrapped_pairs(i - 1)
+            wrapped_one(i - 1)
+
+    wrapped_one(hpg - 1)
 
     @pl.loop(0, hpg)
     def _(i):
@@ -438,7 +456,6 @@
         @pl.when(i == 1)
         def _():
             pass_back(hpg - 1)
-            wrapped_pairs(hpg - 1)
 
         @pl.when((m <= 1) & (i >= 2))
         def _():
@@ -470,8 +487,8 @@
     @pl.loop(0, hpg)
     def _(i):
         for p in peers:
-            kv_copy(i, *p).wait_send()
-            qg_copy(i, *p).wait_send()
+            for kind in range(2):
+                split_copy(kind, i, *p).wait_send()
             dq_copy(i, *p).wait_send()
             dkv_copy(i, *p).wait_send()
 
@@ -498,13 +515,9 @@
             xq_copy(i, 0).wait_send()
             xq_copy(i, 1).wait_send()
 
-        @pl.when(m == 1)
+        @pl.when(m <= 1)
         def _():
             xq_copy(i, 2).wait_send()
-
-        @pl.when(m == last)
-        def _():
-            xq_hand_on(i).wait_send()
 
         @pl.when(m >= last - 1)
         def _():
@@ -522,6 +535,30 @@
     @pl.when(m == 0)
     def _():
         xl_copy(1).wait_send()
+
+
+PARTS = 2
+
+
+def join_heads(dq_ref, dkv_ref, dq_out, dk_out, dv_out, by_head, by_row, s_load, s_store):
+    groups, hpg, rows, dim = dq_ref.shape
+    size = rows // PARTS
+    loads, stores = [], []
+    for n, src in enumerate((dq_ref, dkv_ref.at[:, :, 0], dkv_ref.at[:, :, 1])):
+        for part in range(PARTS):
+            cut = pl.ds(part * size, size)
+            loads.append(pltpu.make_async_copy(src.at[:, :, cut], by_head.at[n, :, :, cut], s_load.at[n, part]))
+            loads[-1].start()
+    for n, dst in enumerate((dq_out, dk_out, dv_out)):
+        for part in range(PARTS):
+            cut = pl.ds(part * size, size)
+            loads[n * PARTS + part].wait()
+            block = by_head[n, :, :, part * size : (part + 1) * size].reshape(groups * hpg, size, dim)
+            by_row[n, part * size : (part + 1) * size] = jnp.swapaxes(block, 0, 1)
+            stores.append(pltpu.make_async_copy(by_row.at[n, cut], dst.at[cut], s_store.at[n, part]))
+            stores[-1].start()
+    for store in stores:
+        store.wait()
 
 
 def on_device(queries, key_vectors, value_vectors, grad_output, logsumexp, row_delta):
@@ -543,10 +580,8 @@
         in_specs=[hbm] * 6,
         out_specs=(hbm, hbm),
         scratch_shapes=[
-            pltpu.VMEM((GROUP, hpg, 2, rows, dim), BF16),
-            pltpu.VMEM((GROUP, hpg, 2, rows, dim), BF16),
-            pltpu.VMEM((hpg, GROUP, 2, rows, dim), BF16),
-            pltpu.VMEM((hpg, GROUP, 2, rows, dim), BF16),
+            pltpu.VMEM((2, GROUP, hpg, 2, rows, dim), BF16),
+            pltpu.VMEM((2, hpg, GROUP, 2, rows, dim), BF16),
             pltpu.VMEM((2, 2, *logsumexp.shape), F32),
             pltpu.VMEM((hpg, 3, 2, 2, rows, dim), BF16),
             pltpu.VMEM((hpg, 3, 2, half, dim), BF16),
@@ -565,7 +600,7 @@
             pltpu.SemaphoreType.REGULAR,
             dma((6,)),
             dma((hpg, 2)),
-            *[dma((hpg, GROUP - 1))] * 4,
+            *[dma((2, hpg, GROUP - 1))] * 2,
             *[dma((1,))] * 2,
             *[dma((hpg, 3))] * 4,
             *[dma((hpg, GROUP - 1))] * 4,
@@ -579,10 +614,21 @@
         name="window_grads",
     )(queries, key_vectors, value_vectors, grad_output, logsumexp, row_delta)
 
-    def by_row(x):
-        return jnp.swapaxes(x.reshape(heads, rows, dim), 0, 1)
-
-    return by_row(dq), by_row(dkv[:, :, 0]), by_row(dkv[:, :, 1])
+    out = jax.ShapeDtypeStruct((rows, heads, dim), BF16)
+    return pl.pallas_call(
+        join_heads,
+        out_shape=(out, out, out),
+        in_specs=[hbm] * 2,
+        out_specs=(hbm, hbm, hbm),
+        scratch_shapes=[
+            pltpu.VMEM((3, GROUP, hpg, rows, dim), BF16),
+            pltpu.VMEM((3, rows, heads, dim), BF16),
+            dma((3, PARTS)),
+            dma((3, PARTS)),
+        ],
+        compiler_params=pltpu.CompilerParams(vmem_limit_bytes=60 << 20),
+        name="join_heads",
+    )(dq, dkv)
 
 
 def solution(mesh):

time: 66.9 us -> 62.5 us (0.934)
  local copies, waits for them, and re-layouts: 4 us -> 0 us
    pallas_call x1, Pallas kernels: 62.1 us -> 59.4 us  [on_device(): pl.pallas_call(body, out_shape=(dq_shape, dkv_shape), in_specs=[hbm] * 6,...]
    pallas_call x0 -> x1, Pallas kernels: none -> 2.31 us  [on_device(): pl.pallas_call(join_heads, out_shape=(out, out, out), in_specs=[hbm] * 2,...]
    reshape x1 -> x0, local copies, waits for them, and re-layouts: 2.26 us -> none  [by_row(): return jnp.swapaxes(x.reshape(heads, rows, dim), 0, 1)]
    transpose x1 -> x0, local copies, waits for them, and re-layouts: 1.64 us -> none  [by_row(): return jnp.swapaxes(x.reshape(heads, rows, dim), 0, 1)]
where the time goes in v3:
time: 62.5 us; the launch traced here: 62.3 us
  Pallas kernels  61.7 us (99%)
  between operations  0.64 us (1%)
    pallas_call x1, Pallas kernels, on_device(): pl.pallas_call(body, out_shape=(dq_shape, dkv_shape), in_specs=[hbm] * 6,...  59.4 us
    pallas_call x1, Pallas kernels, on_device(): pl.pallas_call(join_heads, out_shape=(out, out, out), in_specs=[hbm] * 2,...  2.31 us

profile of v3, /device:TPU:1, one launch (start us, length us, event | category | flops | bytes accessed | tf_op | source)
XLA Modules:
  0.0 62.3 jit_solution(3383419945642022237)
XLA Ops:
  0.6 59.4 %window_grads.1 = (bf16[8,4,64,128]{3,2,1,0:T(8,128)(2,1)}, bf16[8,4,2,64,128]{4,3,2,1,0:T(8,128)(2,1)}) custom-call(bf16[64,32,128]{2,1,0:T(8,128)(2,1)} %refs_0_.1, bf16[64,32,128]{2,1,0:T(8,128)(2,1)} %refs_1_.1, bf16[64,32,128]{2,1,0:T(8,128)(2,1)} %refs_2_.1, bf16[64,32,128]{2,1,0:T(8,128)(2,1)} %refs_3_.1, f32[8,256]{1,0:T(8,128)} %refs_4_.1, ...), custom_call_target="tpu_custom_call" | custom-call | tf_op jit(solution)/shard_map/window_grads/pallas_call | solution.py:577
  60.0 2.3 %join_heads.1 = (bf16[64,32,128]{2,1,0:T(8,128)(2,1)}, bf16[64,32,128]{2,1,0:T(8,128)(2,1)}, bf16[64,32,128]{2,1,0:T(8,128)(2,1)}) custom-call(bf16[8,4,64,128]{3,2,1,0:T(8,128)(2,1)} %get-tuple-element.5.dq_ref, bf16[8,4,2,64,128]{4,3,2,1,0:T(8,128)(2,1)} %get-tuple-element.6.dkv_ref), custom_call_target="tpu_custom_call" | custom-call | tf_op jit(solution)/shard_map/join_heads/pallas_call | solution.py:618

commit v4 on v3

--- a/solution.py
+++ b/solution.py
@@ -43,7 +43,7 @@
         lo2, hi2, core2 = (lo + o % 2) % 2, (hi + o // 2 % 2) % 2, (core + o // 4) % 2
         return (2 * m + lo2, hi2 * 2 + core2), lo2 * 4 + hi2 * 2 + core2, hi2 * 4 + core2 * 2 + lo2
 
-    peers = [(o, *peer(o)) for o in (2, 6, 3, 7, 1, 5, 4)]
+    peers = [(o, *peer(o)) for o in (2, 3, 1, 6, 7, 5, 4)]
 
     def row(step):
         return (2 * ((m + step + rows_total) % rows_total) + lo, h)
@@ -86,7 +86,7 @@
         )
 
     def stat_copy():
-        return copy(stats.at[lo], stats.at[lo], s_st.at[0], r_st.at[0], peers[4][1])
+        return copy(stats.at[lo], stats.at[lo], s_st.at[0], r_st.at[0], peer(1)[0])
 
     def halo_copy(i, n):
         src = halo.at[i, 2] if n == 0 else kv_buf.at[i, pl.ds((0, 4)[n - 1], 2)]
@@ -220,7 +220,7 @@
             def _():
                 halo_copy(i, 0).start()
 
-    def share(i):
+    def share_keys(i):
         split_arrived(0, i, 0)
 
         @pl.when(m <= last - 1)
@@ -228,6 +228,7 @@
             halo_copy(i, 2).start()
             halo_copy(i, 1).start()
 
+    def share_queries(i):
         split_arrived(1, i, 1)
 
         @pl.when(m == 0)
@@ -235,9 +236,21 @@
             xq_copy(i, 0).start()
             xq_copy(i, 1).start()
 
-        @pl.when(m <= 1)
+        @pl.when(m == 1)
         def _():
             xq_copy(i, 2).start()
+
+        @pl.when((m == 0) & (i >= 1))
+        def _():
+            xq_copy(i - 1, 2).start()
+
+        @pl.when((m == 0) & (i == hpg - 1))
+        def _():
+            xq_copy(i, 2).start()
+
+    @pl.loop(0, 2)
+    def _(i):
+        share_keys(i)
 
     stat_copy().wait_recv()
 
@@ -252,7 +265,7 @@
 
     @pl.loop(0, 2)
     def _(i):
-        share(i)
+        share_queries(i)
 
     @pl.loop(0, 2)
     def _(i):
@@ -441,7 +454,8 @@
 
         @pl.when(i + 2 < hpg)
         def _():
-            share(i + 2)
+            share_keys(i + 2)
+            share_queries(i + 2)
 
         @pl.when(i >= 1)
         def _():

time: 62.5 us -> 61.6 us (0.986)
  Pallas kernels: 61.7 us -> 60.8 us
    pallas_call x1, Pallas kernels: 59.4 us -> 58.5 us  [on_device(): pl.pallas_call(body, out_shape=(dq_shape, dkv_shape), in_specs=[hbm] * 6,...]
where the time goes in v4:
time: 61.6 us; the launch traced here: 61.4 us
  Pallas kernels  60.8 us (99%)
  between operations  0.64 us (1%)
    pallas_call x1, Pallas kernels, on_device(): pl.pallas_call(body, out_shape=(dq_shape, dkv_shape), in_specs=[hbm] * 6,...  58.5 us
    pallas_call x1, Pallas kernels, on_device(): pl.pallas_call(join_heads, out_shape=(out, out, out), in_specs=[hbm] * 2,...  2.31 us

profile of v4, /device:TPU:1, one launch (start us, length us, event | category | flops | bytes accessed | tf_op | source)
XLA Modules:
  0.0 61.4 jit_solution(6874592611271146716)
XLA Ops:
  0.6 58.5 %window_grads.1 = (bf16[8,4,64,128]{3,2,1,0:T(8,128)(2,1)}, bf16[8,4,2,64,128]{4,3,2,1,0:T(8,128)(2,1)}) custom-call(bf16[64,32,128]{2,1,0:T(8,128)(2,1)} %refs_0_.1, bf16[64,32,128]{2,1,0:T(8,128)(2,1)} %refs_1_.1, bf16[64,32,128]{2,1,0:T(8,128)(2,1)} %refs_2_.1, bf16[64,32,128]{2,1,0:T(8,128)(2,1)} %refs_3_.1, f32[8,256]{1,0:T(8,128)} %refs_4_.1, ...), custom_call_target="tpu_custom_call" | custom-call | tf_op jit(solution)/shard_map/window_grads/pallas_call | solution.py:591
  59.1 2.3 %join_heads.1 = (bf16[64,32,128]{2,1,0:T(8,128)(2,1)}, bf16[64,32,128]{2,1,0:T(8,128)(2,1)}, bf16[64,32,128]{2,1,0:T(8,128)(2,1)}) custom-call(bf16[8,4,64,128]{3,2,1,0:T(8,128)(2,1)} %get-tuple-element.5.dq_ref, bf16[8,4,2,64,128]{4,3,2,1,0:T(8,128)(2,1)} %get-tuple-element.6.dkv_ref), custom_call_target="tpu_custom_call" | custom-call | tf_op jit(solution)/shard_map/join_heads/pallas_call | solution.py:632

commit v5 on v4

--- a/solution.py
+++ b/solution.py
@@ -343,6 +343,13 @@
         for p in peers:
             dq_copy(i, *p).start()
 
+    def send_dq_part(i, part):
+        for p in peers:
+
+            @pl.when(p[2] // 2 % 2 == part)
+            def _(p=p):
+                dq_copy(i, *p).start()
+
     def pass_back(i):
         @pl.when(m >= 1)
         def _():
@@ -403,7 +410,7 @@
                 more = xd_in[i, slot].astype(F32).reshape(2, rows, dim)
                 dq_buf[i, at] = (dq_buf[i, at].astype(F32) + more).astype(BF16)
 
-        send_dq(i)
+        send_dq_part(i, 1)
 
     @pl.when(m == last)
     def _():
@@ -438,6 +445,10 @@
         def _():
             send_dq(i)
 
+        @pl.when(m <= 1)
+        def _():
+            send_dq_part(i, 0)
+
     @pl.loop(0, hpg)
     def _(i):
         split_arrived(0, i, 1)
@@ -467,7 +478,7 @@
     def _(i):
         finish(i)
 
-        @pl.when(i == 1)
+        @pl.when(i == 0)
         def _():
             pass_back(hpg - 1)
 

time: 61.6 us -> 60.2 us (0.977)
  the two profiles are of different devices: /device:TPU:1 before, /device:TPU:7 now
where the time goes in v5:
time: 60.2 us; the launch traced here: 60 us
  Pallas kernels  59.4 us (99%)
  between operations  0.64 us (1%)
    pallas_call x1, Pallas kernels, on_device(): pl.pallas_call(body, out_shape=(dq_shape, dkv_shape), in_specs=[hbm] * 6,...  57 us
    pallas_call x1, Pallas kernels, on_device(): pl.pallas_call(join_heads, out_shape=(out, out, out), in_specs=[hbm] * 2,...  2.31 us

profile of v5, /device:TPU:7, one launch (start us, length us, event | category | flops | bytes accessed | tf_op | source)
XLA Modules:
  0.0 60.0 jit_solution(5144921252481099896)
XLA Ops:
  0.6 57.0 %window_grads.1 = (bf16[8,4,64,128]{3,2,1,0:T(8,128)(2,1)}, bf16[8,4,2,64,128]{4,3,2,1,0:T(8,128)(2,1)}) custom-call(bf16[64,32,128]{2,1,0:T(8,128)(2,1)} %refs_0_.1, bf16[64,32,128]{2,1,0:T(8,128)(2,1)} %refs_1_.1, bf16[64,32,128]{2,1,0:T(8,128)(2,1)} %refs_2_.1, bf16[64,32,128]{2,1,0:T(8,128)(2,1)} %refs_3_.1, f32[8,256]{1,0:T(8,128)} %refs_4_.1, ...), custom_call_target="tpu_custom_call" | custom-call | tf_op jit(solution)/shard_map/window_grads/pallas_call | solution.py:602
  57.7 2.3 %join_heads.1 = (bf16[64,32,128]{2,1,0:T(8,128)(2,1)}, bf16[64,32,128]{2,1,0:T(8,128)(2,1)}, bf16[64,32,128]{2,1,0:T(8,128)(2,1)}) custom-call(bf16[8,4,64,128]{3,2,1,0:T(8,128)(2,1)} %get-tuple-element.5.dq_ref, bf16[8,4,2,64,128]{4,3,2,1,0:T(8,128)(2,1)} %get-tuple-element.6.dkv_ref), custom_call_target="tpu_custom_call" | custom-call | tf_op jit(solution)/shard_map/join_heads/pallas_call | solution.py:643
